TPU v7x, 512 devices: a whole 4x4x16 slice. The times are simulated.
512 devices in a mesh: lat: 128 (over x_hi, z, y), chan: 4 (over x_lo, core).
Axes of the slice: x: 4 (x_hi: 2, x_lo: 2; x = x_hi * 2 + x_lo), y: 4, z: 16, core: 2. Of those that a mesh axis runs over, the one named last changes fastest.
Arguments:
- input_field: bfloat16 [128, 384, 3072], P('lat', 'chan'), may hold values from -100 to 100
- cotangent: bfloat16 [128, 384, 3072], P('lat', 'chan'), may hold values from -6 to 6
- norm_gain: float32 [384], P('chan'), may hold values from 0.1 to 1.9
- inner_weights: bfloat16 [4, 2, 96, 96], P('chan'), may hold values from -0.4375 to 0.4375
- inner_bias: float32 [4, 2, 96], P('chan'), may hold values from -6 to 6
- outer_weights: bfloat16 [4, 2, 96, 96], P('chan'), may hold values from -0.4375 to 0.4375
- keep_codes: int32 [128, 1536, 384], P(None, 'lat', 'chan'), may hold values from 0 to 15
Outputs:
- grad_input: bfloat16 [128, 384, 3072], P('lat', 'chan')
- grad_inner_weights: float32 [4, 2, 96, 96], P('chan')
- grad_inner_bias: float32 [4, 2, 96], P('chan')
- grad_outer_weights: float32 [4, 2, 96, 96], P('chan')
- grad_outer_bias: float32 [4, 2, 96], P('chan')
- grad_gain: float32 [384], P('chan')
Inputs may be any that keep to these rules, and one draw needn't show every extreme that they name: `keep_codes`: bits 0 and 1 belong to the hidden unit's real and imaginary part, bits 2 and 3 to the output channel's.
All inputs are finite; a program needn't handle non-finite values.
Results may differ from a plain program's by a relative error of at most 0.01.
Values may be sent and summed in bfloat16 or wider, within the bound.
A program may use at most 64 MiB of HBM per device.

v0:
```python
import math

import jax
import jax.numpy as jnp
from jax import lax
from jax.sharding import PartitionSpec as P

WP = 24


exact_mode = lax.Precision.HIGHEST


def angle_table(count_rows, count_cols, period):
    product = (
        jnp.outer(jnp.arange(count_rows, dtype=jnp.int32), jnp.arange(count_cols, dtype=jnp.int32))
        % period
    )
    angles = product.astype(jnp.float32) * (2.0 * math.pi / period)
    return (jnp.cos(angles), jnp.sin(angles))


def longitude_forward(values, factor_p):
    lat_rows, channels, lon_width = values.shape
    factor_q = lon_width // factor_p
    grid_view = values.reshape(lat_rows, channels, factor_p, factor_q)
    cos_small, sin_small = angle_table(factor_p, factor_p, factor_p)
    first_real = jnp.einsum("lcpq,pa->lcaq", grid_view, cos_small, precision=exact_mode)
    first_imag = -jnp.einsum("lcpq,pa->lcaq", grid_view, sin_small, precision=exact_mode)
    cos_turn, sin_turn = angle_table(factor_p, factor_q, lon_width)
    turn_real = first_real * cos_turn + first_imag * sin_turn
    turn_imag = first_imag * cos_turn - first_real * sin_turn
    cos_large, sin_large = angle_table(factor_q, factor_q // 2, factor_q)
    out_real = jnp.einsum("lcaq,qj->ljac", turn_real, cos_large, precision=exact_mode) + jnp.einsum(
        "lcaq,qj->ljac", turn_imag, sin_large, precision=exact_mode
    )
    out_imag = jnp.einsum("lcaq,qj->ljac", turn_imag, cos_large, precision=exact_mode) - jnp.einsum(
        "lcaq,qj->ljac", turn_real, sin_large, precision=exact_mode
    )
    norm_scale = 1.0 / math.sqrt(lon_width)
    mode_count = lon_width // 2
    return (
        out_real.reshape(lat_rows, mode_count, channels) * norm_scale,
        out_imag.reshape(lat_rows, mode_count, channels) * norm_scale,
    )


def longitude_inverse(real_part, imag_part, factor_p):
    lat_rows, mode_count, channels = real_part.shape
    lon_width = 2 * mode_count
    factor_q = lon_width // factor_p
    real_grid = real_part.reshape(lat_rows, factor_q // 2, factor_p, channels)
    imag_grid = imag_part.reshape(lat_rows, factor_q // 2, factor_p, channels)
    cos_large, sin_large = angle_table(factor_q // 2, factor_q, factor_q)
    mid_real = jnp.einsum("ljac,jq->lcaq", real_grid, cos_large, precision=exact_mode) - jnp.einsum(
        "ljac,jq->lcaq", imag_grid, sin_large, precision=exact_mode
    )
    mid_imag = jnp.einsum("ljac,jq->lcaq", imag_grid, cos_large, precision=exact_mode) + jnp.einsum(
        "ljac,jq->lcaq", real_grid, sin_large, precision=exact_mode
    )
    cos_turn, sin_turn = angle_table(factor_p, factor_q, lon_width)
    turned_real = mid_real * cos_turn - mid_imag * sin_turn
    turned_imag = mid_real * sin_turn + mid_imag * cos_turn
    cos_small, sin_small = angle_table(factor_p, factor_p, factor_p)
    result = jnp.einsum("lcaq,ap->lcpq", turned_real, cos_small, precision=exact_mode) - jnp.einsum(
        "lcaq,ap->lcpq", turned_imag, sin_small, precision=exact_mode
    )
    return result.reshape(lat_rows, channels, lon_width) * (1.0 / math.sqrt(lon_width))


def latitude_transform(real_part, imag_part, inverse):
    lat_total = real_part.shape[0]
    cos_lat, sin_lat = angle_table(lat_total, lat_total, lat_total)
    norm_scale = 1.0 / math.sqrt(lat_total)

    def lat_sum(table_vals, values):
        return jnp.einsum("mh,hkc->mkc", table_vals, values, precision=exact_mode)

    if inverse:
        out_real = lat_sum(cos_lat, real_part) - lat_sum(sin_lat, imag_part)
        out_imag = lat_sum(cos_lat, imag_part) + lat_sum(sin_lat, real_part)
    else:
        out_real = lat_sum(cos_lat, real_part) + lat_sum(sin_lat, imag_part)
        out_imag = lat_sum(cos_lat, imag_part) - lat_sum(sin_lat, real_part)
    return (out_real * norm_scale, out_imag * norm_scale)


def complex_matrix(weight_pair):
    real_part = weight_pair[0]
    imag_part = weight_pair[1]
    top_rows = jnp.concatenate([real_part, imag_part], axis=1)
    bottom_rows = jnp.concatenate([-imag_part, real_part], axis=1)
    return jnp.concatenate([top_rows, bottom_rows], axis=0)


def split_gradient(product, half_size):
    real_grad = product[:half_size, :half_size] + product[half_size:, half_size:]
    imag_grad = product[:half_size, half_size:] - product[half_size:, :half_size]
    return jnp.stack([real_grad, imag_grad])


def code_bit(code_rows, bit_place):
    return jnp.bitwise_and(jnp.right_shift(code_rows, bit_place), 1).astype(jnp.float32)


def per_device(
    input_field, cotangent, norm_gain, inner_weights, inner_bias, outer_weights, keep_codes
):
    lat_rows, channels, lon_width = input_field.shape
    mode_count = lon_width // 2
    block_width = inner_weights.shape[2]
    all_channels = channels * lax.axis_size("chan")
    mode_ids = jnp.arange(mode_count, dtype=jnp.int32)
    cot_weight = jnp.where(mode_ids == 0, 1.0, 2.0).astype(jnp.float32)[None, :, None]
    gain_col = norm_gain[None, :, None]

    def to_slab(values, weight):
        slab_real, slab_imag = longitude_forward(values, WP)
        return jnp.concatenate([slab_real * weight, slab_imag * weight], axis=2).astype(
            jnp.bfloat16
        )

    source = input_field.astype(jnp.float32)
    chan_total = lax.psum(jnp.sum(source, axis=1), "chan")
    centre = (chan_total / all_channels)[:, None, :]
    offset = source - centre
    spread = lax.psum(jnp.sum(offset * offset, axis=1), "chan")
    variance = spread / all_channels
    inv_std = lax.rsqrt(variance + 1e-05)[:, None, :]
    normed = offset * inv_std
    pencil_in, pencil_cot = (
        lax.all_to_all(
            to_slab(normed * gain_col, 1.0), "lat", split_axis=1, concat_axis=0, tiled=True
        ),
        lax.all_to_all(
            to_slab(cotangent.astype(jnp.float32), cot_weight),
            "lat",
            split_axis=1,
            concat_axis=0,
            tiled=True,
        ),
    )
    all_lat = pencil_in.shape[0]
    local_modes = pencil_in.shape[1]
    flat_rows = all_lat * local_modes
    wide_in = pencil_in.astype(jnp.float32)
    in_real, in_imag = latitude_transform(wide_in[..., :channels], wide_in[..., channels:], False)
    in_real = in_real.astype(jnp.bfloat16)
    in_imag = in_imag.astype(jnp.bfloat16)
    wide_cot = pencil_cot.astype(jnp.float32)
    cot_real, cot_imag = latitude_transform(
        wide_cot[..., :channels], wide_cot[..., channels:], False
    )
    grad_scale = 1.0 / math.sqrt(all_lat * mode_count)
    freq_rows = jnp.concatenate([in_real, in_imag], axis=2).reshape(flat_rows, 2 * block_width)
    cot_rows = jnp.concatenate([cot_real, cot_imag], axis=2).reshape(flat_rows, 2 * block_width)
    code_rows = keep_codes.reshape(flat_rows, block_width)
    relu_keep = jnp.concatenate([code_bit(code_rows, 0), code_bit(code_rows, 1)], axis=1)
    shrink_keep = jnp.concatenate([code_bit(code_rows, 2), code_bit(code_rows, 3)], axis=1)
    shrink_grad = (cot_rows * shrink_keep).astype(jnp.bfloat16)
    first_matrix = complex_matrix(inner_weights[0])
    second_matrix = complex_matrix(outer_weights[0])
    bias_row = inner_bias[0].reshape(2 * block_width)
    hidden = (
        (jnp.dot(freq_rows, first_matrix, preferred_element_type=jnp.float32) + bias_row)
        * relu_keep
    ).astype(jnp.bfloat16)
    outer_product = jnp.dot(hidden.T, shrink_grad, preferred_element_type=jnp.float32)
    back_hidden = (
        jnp.dot(shrink_grad, second_matrix.T, preferred_element_type=jnp.float32) * relu_keep
    ).astype(jnp.bfloat16)
    inner_product = jnp.dot(freq_rows.T, back_hidden, preferred_element_type=jnp.float32)
    grad_rows = jnp.dot(back_hidden, first_matrix.T, preferred_element_type=jnp.float32).reshape(
        all_lat, local_modes, 2 * block_width
    )
    inner_grads = [split_gradient(inner_product, block_width) * grad_scale]
    inner_shifts = [
        jnp.sum(back_hidden.astype(jnp.float32), axis=0).reshape(2, block_width) * grad_scale
    ]
    outer_grads = [split_gradient(outer_product, block_width) * grad_scale]
    outer_shifts = [
        jnp.sum(shrink_grad.astype(jnp.float32), axis=0).reshape(2, block_width) * grad_scale
    ]
    real_pieces = grad_rows[..., :block_width]
    imag_pieces = grad_rows[..., block_width:]
    inner_local = jnp.stack(inner_grads)
    ishift_local = jnp.stack(inner_shifts)
    outer_local = jnp.stack(outer_grads)
    oshift_local = jnp.stack(outer_shifts)
    back_real, back_imag = latitude_transform(real_pieces, imag_pieces, True)
    back_pencil = jnp.concatenate([back_real, back_imag], axis=2).astype(jnp.bfloat16)
    back_slab = lax.all_to_all(back_pencil, "lat", split_axis=0, concat_axis=1, tiled=True).astype(
        jnp.float32
    )
    grad_norm = longitude_inverse(back_slab[..., :channels], back_slab[..., channels:], WP)
    gain_scale = 1.0 / math.sqrt(all_lat * lon_width)
    gain_local = jnp.sum(grad_norm * normed, axis=(0, 2)) * gain_scale
    grad_hat = grad_norm * gain_col
    hat_sum, cross_sum = lax.psum(
        (jnp.sum(grad_hat, axis=1), jnp.sum(grad_hat * normed, axis=1)), "chan"
    )
    grad_input = (
        (
            grad_hat
            - (hat_sum / all_channels)[:, None, :]
            - normed * (cross_sum / all_channels)[:, None, :]
        )
        * inv_std
    ).astype(jnp.bfloat16)
    inner_sum, inner_bias_sum, outer_sum, outer_bias_sum, gain_sum = lax.psum(
        (inner_local, ishift_local, outer_local, oshift_local, gain_local), "lat"
    )
    return (grad_input, inner_sum, inner_bias_sum, outer_sum, outer_bias_sum, gain_sum)


def solution(mesh):
    in_specs = (
        P("lat", "chan", None),
        P("lat", "chan", None),
        P("chan"),
        P("chan", None, None, None),
        P("chan", None, None),
        P("chan", None, None, None),
        P(None, "lat", "chan"),
    )
    out_specs = (
        P("lat", "chan", None),
        P("chan", None, None, None),
        P("chan", None, None),
        P("chan", None, None, None),
        P("chan", None, None),
        P("chan"),
    )
    return jax.shard_map(
        per_device, mesh=mesh, in_specs=in_specs, out_specs=out_specs, check_vma=False
    )
```

profile of v0, /device:TPU:2, one launch (start us, length us, event | category | flops | bytes accessed | tf_op | source)
XLA Modules:
  0.0 1521.4 jit_solution(17227120026294030052)
XLA Ops:
  10.0 2.7 fusion.45
  12.8 2.8 fusion.41
  15.5 2.8 fusion.18
  18.7 2.7 fusion.17
  22.6 9.1 copy.141
  32.2 8.9 reduce.10
  41.1 1.8 reshape.576
  42.8 22.0 %all-to-all-start = ((bf16[128,2,1152]{2,1,0:T(2,128)(2,1)}), bf16[128,2,1152]{2,1,0:T(2,128)(2,1)}, u32[]{:S(2)}, u32[]{:S(2)}) async-start(bf16[128,2,1152]{2,1,0:T(2,128)(2,1)} %reshape.576), calls=%async_computation | async-start | bytes 1179648 | tf_op jit(solution)/shard_map/all_to_all | solution.py:135
  75.7 28.3 %all-to-all-done = bf16[128,2,1152]{2,1,0:T(2,128)(2,1)} async-done(((bf16[128,2,1152]{2,1,0:T(2,128)(2,1)}), bf16[128,2,1152]{2,1,0:T(2,128)(2,1)}, u32[]{:S(2)}, u32[]{:S(2)}) %all-to-all-start) | async-done | bytes 589856 | tf_op jit(solution)/shard_map/all_to_all | solution.py:135
  104.0 5.3 reshape.577
  109.3 8.2 bitcast_reduce_fusion.1
  126.3 2.2 fusion.3
  131.8 1.9 reshape.534
  140.7 1.9 copy.78
  142.7 6.3 all-to-all-start.1
  149.2 10.7 psum.64
  160.1 10.9 psum.65
  171.1 35.5 %all-to-all-done.1 = bf16[128,12,192]{2,1,0:T(8,128)(2,1)S(1)} async-done(((bf16[128,12,192]{2,1,0:T(8,128)(2,1)}), bf16[128,12,192]{2,1,0:T(8,128)(2,1)S(1)}, u32[]{:S(2)}, u32[]{:S(2)}) %all-to-all-start.1) | async-done | bytes 589856 | tf_op jit(solution)/shard_map/all_to_all | solution.py:192
  217.5 2.9 fusion.35
  220.5 2.8 fusion.39
  223.2 2.8 fusion.22
  226.2 2.8 fusion.23
  229.6 8.9 copy.140
  238.5 9.8 reduce.11
  248.3 3.1 reshape.578
  251.4 6.4 all-to-all-start.2
  258.1 10.9 all-reduce.2
  270.2 24.8 %all-to-all-done.2 = bf16[128,2,1152]{2,1,0:T(2,128)(2,1)S(1)} async-done(((bf16[128,2,1152]{2,1,0:T(2,128)(2,1)}), bf16[128,2,1152]{2,1,0:T(2,128)(2,1)S(1)}, u32[]{:S(2)}, u32[]{:S(2)}) %all-to-all-start.2) | async-done | bytes 589856 | tf_op jit(solution)/shard_map/all_to_all | solution.py:132
  296.0 8.2 bitcast_reduce_fusion
  311.8 1.9 fusion.19
  315.2 353.0 %all-reduce = (f32[1,2,96]{2,1,0:T(2,128)}, f32[1,2,96]{2,1,0:T(2,128)}, f32[96]{0:T(128)}) all-reduce(f32[1,2,96]{2,1,0:T(2,128)S(1)} %mul.876, f32[1,2,96]{2,1,0:T(2,128)S(1)} %mul.881, f32[96]{0:T(128)S(1)} %broadcast_multiply_fusion.5), channel_id=1, replica_groups=mesh['lat'=128,'chan'=4] {'lat'}, use_global_device_ids=true, to_apply=%region_10.11 | all-reduce | flops 480 | bytes 3840 | tf_op jit(solution)/shard_map/psum | solution.py:210
  668.2 842.9 %all-reduce.5.cloned.1.call-done = (f32[1,2,96,96]{3,2,1,0:T(8,128)}, f32[1,2,96,96]{3,2,1,0:T(8,128)}) async-done(((f32[1,2,96,96]{3,2,1,0:T(8,128)}, f32[1,2,96,96]{3,2,1,0:T(8,128)}), (f32[1,2,96,96]{3,2,1,0:T(8,128)}, f32[1,2,96,96]{3,2,1,0:T(8,128)})) %all-reduce.5.cloned.1.call-update) | async-done | bytes 147472 | tf_op jit(solution)/shard_map/psum | solution.py:210
  (147 shorter events, 61.1 us)
Async XLA Ops:
  7.2 1.9 copy-start.10
  41.1 23.8 %copy-start.6 = (s32[128,12,96]{0,2,1:T(8,128)S(1)}, s32[128,12,96]{0,2,1:T(8,128)}, u32[]{:S(2)}) copy-start(s32[128,12,96]{0,2,1:T(8,128)} %param.13) | copy-start | bytes 1769476
  42.8 61.2 %all-to-all-start = ((bf16[128,2,1152]{2,1,0:T(2,128)(2,1)}), bf16[128,2,1152]{2,1,0:T(2,128)(2,1)}, u32[]{:S(2)}, u32[]{:S(2)}) async-start(bf16[128,2,1152]{2,1,0:T(2,128)(2,1)} %reshape.576), calls=%async_computation | async-start | bytes 1179648 | tf_op jit(solution)/shard_map/all_to_all | solution.py:135
  72.3 1.0 copy-start.12
  72.3 1.6 copy-start.13
  124.9 1.4 copy-start.1
  126.2 2.2 copy-start.7
  126.2 2.2 copy-start.9
  126.2 2.2 copy-start.17
  126.2 2.2 copy-start.18
  126.3 2.2 copy-start.19
  128.4 0.9 copy-start.4
  128.5 1.7 copy-start.14
  128.5 1.6 copy-start.15
  128.5 1.6 copy-start.16
  129.3 0.8 copy-start.2
  142.7 6.3 copy-start.20
  142.7 6.4 copy-start
  142.7 28.4 %copy-start.21 = (f32[96]{0:T(128)S(1)}, f32[96]{0:T(128)}, u32[]{:S(2)}) copy-start(f32[96]{0:T(128)} %param.9) | copy-start | bytes 1156
  142.7 63.9 %all-to-all-start.1 = ((bf16[128,12,192]{2,1,0:T(8,128)(2,1)}), bf16[128,12,192]{2,1,0:T(8,128)(2,1)S(1)}, u32[]{:S(2)}, u32[]{:S(2)}) async-start(bf16[128,12,192]{2,1,0:T(8,128)(2,1)} %copy.78), calls=%async_computation.1 | async-start | bytes 2097152 | tf_op jit(solution)/shard_map/all_to_all | solution.py:192
  208.8 0.8 copy-start.11
  251.4 43.6 %all-to-all-start.2 = ((bf16[128,2,1152]{2,1,0:T(2,128)(2,1)}), bf16[128,2,1152]{2,1,0:T(2,128)(2,1)S(1)}, u32[]{:S(2)}, u32[]{:S(2)}) async-start(bf16[128,2,1152]{2,1,0:T(2,128)(2,1)} %reshape.578), calls=%async_computation.2 | async-start | bytes 1179648 | tf_op jit(solution)/shard_map/all_to_all | solution.py:132
  257.8 1253.2 %all-reduce.5.cloned.1.call-start = ((), (), s32[]{:S(2)}) async-start(), calls=%async_computation.3 | async-start | bytes 393216 | tf_op jit(solution)/shard_map/psum | solution.py:210
  309.5 1.1 copy-start.3
  310.5 1.1 copy-start.5
  310.5 1.3 copy-start.8
Sparse Core Ops, SparseCore 0:
  315.3 1195.7 all-reduce.4
where the time goes:
time: 1530 us; the launch traced here: 1520 us
  waiting for transfers between devices  931 us (61%)
  blocking collectives  386 us (25%)
  local copies, waits for them, and re-layouts  79.6 us (5%)
  matrix products  46.1 us (3%)
  starting transfers between devices  34.8 us (2%)
  other arithmetic  28.6 us (2%)
  between operations  15.3 us (1%)
    psum x1, waiting for transfers between devices, per_device(): lax.psum((inner_local, ishift_local, outer_local, oshift_local, gain_loca...  843 us
    psum x1, blocking collectives, per_device(): lax.psum((inner_local, ishift_local, outer_local, oshift_local, gain_loca...  353 us
    all_to_all x1, waiting for transfers between devices, per_device(): lax.all_to_all(back_pencil, 'lat', split_axis=0, concat_axis=1, tiled=True)  35.5 us
  transfers between devices with their start and end apart: 4, of which 4 were waited for; matrix products, arithmetic and copies ran while one was open for 1% of the time, Pallas kernels for 0%

commit v1 on v0

v1 whole, which is shorter than its diff:
```python
import math

import jax
import jax.numpy as jnp
import ml_dtypes
import numpy as np
from jax import lax
from jax.experimental import pallas as pl
from jax.experimental.pallas import tpu as pltpu
from jax.sharding import PartitionSpec as P

MESH = pl.DeviceIdType.MESH
BF = jnp.bfloat16
F32 = jnp.float32

LON = 3072
PT = 12
QT = 256
LAT = 128
CH = 96
ALL_CH = 384
NZ = 16
NJ = 8
CK = 3
MC = PT // CK
LC = MC * CH
LP = MC * 128
RW = 56
NP_ = RW // 8


def tables():
    z, p, j = np.meshgrid(np.arange(NZ), np.arange(2), np.arange(NJ), indexing="ij")
    dev = ((j // 4) * 64 + z * 4 + j % 4).reshape(-1)
    part = p.reshape(-1)
    q = np.arange(QT)
    ang = 2 * np.pi * ((dev[:, None] * q[None, :]) % QT) / QT
    cos, sin = np.cos(ang), np.sin(ang)
    re = part[:, None] == 0
    fwd = np.concatenate([np.where(re, cos, -sin), np.where(re, sin, cos)], 1) / math.sqrt(LON)
    inv = np.concatenate([np.where(re, cos, -sin), np.where(re, sin, cos)], 1) / math.sqrt(LON)
    j2, p2, z2 = np.meshgrid(np.arange(NJ), np.arange(2), np.arange(NZ), indexing="ij")
    dev2 = ((j2 // 4) * 64 + z2 * 4 + j2 % 4).reshape(-1)
    part2 = p2.reshape(-1)
    mode = np.arange(LAT)
    ang2 = 2 * np.pi * ((mode[:, None] * dev2[None, :]) % LAT) / LAT
    c2, s2 = np.cos(ang2), np.sin(ang2)
    re2 = part2[None, :] == 0
    lat = np.concatenate([np.where(re2, c2, s2), np.where(re2, -s2, c2)], 0) / math.sqrt(LAT)
    pos = (z2 * 2 * NJ + p2 * NJ + j2).reshape(-1)
    perm = np.zeros((256, 256))
    perm[np.arange(256), pos] = 1.0
    widen = np.zeros((LC, LP))
    for i in range(MC):
        widen[i * CH + np.arange(CH), i * 128 + np.arange(CH)] = 1.0
    turn = 2 * np.pi * np.arange(PT)[:, None] * q[None, :] / LON
    twiddle = np.concatenate([np.cos(turn), np.sin(turn)], 0)
    bf = [a.astype(ml_dtypes.bfloat16) for a in (fwd, inv, lat, lat.T, perm, perm.T, widen, widen.T)]
    return bf + [twiddle.astype(np.float32)]


def real12(u0, u6, s, t):
    h = 0.5
    r3 = math.sqrt(3.0) / 2
    ap, am = u0 + u6, u0 - u6
    s24, d24 = s[2] + s[4], s[2] - s[4]
    s15, d15 = s[1] + s[5], s[1] - s[5]
    e0, o0 = ap + s24, s15 + s[3]
    e1, o1 = am + h * d24, r3 * d15
    e2, o2 = ap - h * s24, h * s15 - s[3]
    real = [e0 + o0, e1 + o1, e2 + o2, am - d24, e2 - o2, e1 - o1, e0 - o0]
    t15, f15 = t[1] + t[5], t[1] - t[5]
    t24, f24 = t[2] + t[4], t[2] - t[4]
    a1, b1 = h * t15 + t[3], r3 * t24
    a2, b2 = r3 * f15, r3 * f24
    imag = [None, -(a1 + b1), -(a2 + b2), t[3] - t15, b2 - a2, b1 - a1, None]
    return real, imag


def dot_nn(a, b):
    return lax.dot_general(a, b, (((1,), (0,)), ((), ())), preferred_element_type=F32)


def dot_nt(a, b):
    return lax.dot_general(a, b, (((1,), (1,)), ((), ())), preferred_element_type=F32)


def dot_tn(a, b):
    return lax.dot_general(a, b, (((0,), (0,)), ((), ())), preferred_element_type=F32)


def kernel(
    x_ref, cot_ref, gain_ref, iw_ref, ib_ref, ow_ref, code_ref,
    fwd_ref, inv_ref, lat_ref, lati_ref, perm_ref, permi_ref, wide_ref, narrow_ref, tw_ref,
    gin_ref, giw_ref, gib_ref, gow_ref, gob_ref, gg_ref,
    ybuf, zs, zr, xs, xr, bxs, bxr, bzs, bzr,
    stat_s, stat_r, tail_s, tail_r, mr, gcol,
    m1, m2, bias, cm, sg_all, bh_all, fi, hd, gp, p1, p2, bsum,
    vbuf, gbuf, hacc, cacc,
    rw, rr1, rs, rr2, rt, rr2b, rr3,
    zs_sem, zr_sem, xs_sem, xr_sem, bxs_sem, bxr_sem, bzs_sem, bzr_sem,
    st_ssem, st_rsem, tl_ssem, tl_rsem,
    r1_ssem, r1_rsem, r2_ssem, r2_rsem, r2b_ssem, r2b_rsem, r3_ssem, r3_rsem,
):
    me = lax.axis_index("lat")
    chan = lax.axis_index("chan")
    x = me // 64
    z = lax.rem(me // 4, NZ)
    y = lax.rem(me, 4)
    j = x * 4 + y
    base_z = me - z * 4

    def z_step(t):
        half = t // 2
        odd = lax.rem(t, 2)
        off = (half + 1) * (1 - odd) + (NZ - 1 - half) * odd
        to = lax.rem(z + off, NZ)
        return to, {"lat": base_z + to * 4}

    def xy_step(t):
        d = t + 1
        tx = lax.rem(x + d // 4, 2)
        ty = lax.rem(y + lax.rem(d, 4), 4)
        return tx * 4 + ty, {"lat": tx * 64 + z * 4 + ty}

    def chan_step(t):
        to = lax.rem(chan + t + 1, 4)
        return to, {"chan": to}

    def each(count, body):
        def one(t, carry):
            body(t)
            return carry

        lax.fori_loop(0, count, one, 0)

    def remote(src, dst, ssem, rsem, to):
        pltpu.make_async_remote_copy(
            src_ref=src, dst_ref=dst, send_sem=ssem, recv_sem=rsem, device_id=to, device_id_type=MESH
        ).start()

    def drain(ref, sem):
        pltpu.make_async_copy(ref, ref, sem).wait()

    def z_exchange(src, dst, ssem, rsem):
        def send(t):
            to, dev = z_step(t)
            remote(src.at[to], dst.at[z], ssem, rsem, dev)

        each(NZ - 1, send)
        dst[z] = src[z]

    def xy_exchange(src, dst, ssem, rsem):
        def send(t):
            to, dev = xy_step(t)
            remote(src.at[to], dst.at[j], ssem, rsem, dev)

        each(NJ - 1, send)
        dst[j] = src[j]

    def xy_share(src, dst, ssem, rsem):
        def send(t):
            _, dev = xy_step(t)
            remote(src, dst.at[j], ssem, rsem, dev)

        each(NJ - 1, send)
        dst[j] = src[...]

    def chan_share(src, dst, ssem, rsem):
        def send(t):
            _, dev = chan_step(t)
            remote(src, dst.at[chan], ssem, rsem, dev)

        each(3, send)
        dst[chan] = src[...]

    def z_done(ref, sem):
        drain(ref.at[pl.ds(0, NZ - 1)], sem)

    def xy_done(ref, sem):
        drain(ref.at[pl.ds(0, NJ - 1)], sem)

    barrier = pltpu.get_barrier_semaphore()

    def greet(step):
        def one(t):
            _, dev = step(t)
            pl.semaphore_signal(barrier, inc=1, device_id=dev, device_id_type=MESH)

        return one

    each(NZ - 1, greet(z_step))
    each(NJ - 1, greet(xy_step))
    each(3, greet(chan_step))

    def lanes(p):
        return slice(p * QT, (p + 1) * QT)

    def forward_rows(load):
        def block(r):
            r0 = pl.multiple_of(r * 16, 16)
            u = [load(r0, p) for p in range(PT)]
            s = [None] + [u[p] + u[PT - p] for p in range(1, 6)]
            t = [None] + [u[p] - u[PT - p] for p in range(1, 6)]
            real, imag = real12(u[0], u[6], s, t)
            for i in range(PT):
                k = i if i <= 6 else PT - i
                yr = real[k]
                yi = imag[k]
                c = tw_ref[i : i + 1, :]
                w = tw_ref[PT + i : PT + i + 1, :]
                if yi is None:
                    ar, ai = yr * c, -(yr * w)
                elif i <= 6:
                    ar, ai = yr * c + yi * w, yi * c - yr * w
                else:
                    ar, ai = yr * c - yi * w, -(yi * c) - yr * w
                rows = pl.ds(pl.multiple_of(i * CH + r0, 16), 16)
                ybuf[rows, 0:QT] = ar.astype(BF)
                ybuf[rows, QT : 2 * QT] = ai.astype(BF)

        each(CH // 16, block)

    def dft_chunk(c):
        return dot_nt(fwd_ref[...], ybuf[pl.ds(c * LC, LC), :])

    forward_rows(lambda r0, p: cot_ref[0, pl.ds(r0, 16), lanes(p)].astype(F32) * 2.0)
    for c in range(CK):
        out = dft_chunk(c)
        if c == 0:
            row = lax.broadcasted_iota(jnp.int32, out.shape, 0)
            lane = lax.broadcasted_iota(jnp.int32, out.shape, 1)
            first = ((row == 0) | (row == NJ)) & (lane < CH)
            out = out * jnp.where(first, 0.5, 1.0)
        zs[0, c] = out.astype(BF).reshape(NZ, 16, LC)
        if c == 0:
            pl.semaphore_wait(barrier, NZ - 1 + NJ - 1 + 3)
        z_exchange(zs.at[0, c], zr.at[0, c], zs_sem.at[0, c], zr_sem.at[0, c])

    for p in range(PT):
        v = x_ref[0, :, lanes(p)].astype(F32)
        total = jnp.sum(v, axis=0, keepdims=True)
        off = v - total * (1.0 / CH)
        r, l = p // 3, (p % 3) * QT
        stat_s[r : r + 1, l : l + QT] = total
        stat_s[4 + r : 5 + r, l : l + QT] = jnp.sum(off * off, axis=0, keepdims=True)
    chan_share(stat_s, stat_r, st_ssem, st_rsem)

    diag = (
        lax.broadcasted_iota(jnp.int32, (CH, CH), 0) == lax.broadcasted_iota(jnp.int32, (CH, CH), 1)
    ).astype(F32)
    gcol[...] = jnp.sum(diag * gain_ref[...], axis=1, keepdims=True)
    for m, w in ((m1, iw_ref), (m2, ow_ref)):
        m[...] = jnp.zeros(m.shape, BF)
        m[0:CH, 0:CH] = w[0, 0]
        m[0:CH, 128 : 128 + CH] = w[0, 1]
        m[128 : 128 + CH, 0:CH] = -w[0, 1]
        m[128 : 128 + CH, 128 : 128 + CH] = w[0, 0]
    bias[...] = jnp.zeros(bias.shape, F32)
    bias[0:1, 0:CH] = ib_ref[0, 0:1, :]
    bias[0:1, 128 : 128 + CH] = ib_ref[0, 1:2, :]
    cm[...] = jnp.zeros(cm.shape, jnp.int32)
    for i in range(PT):
        cm[i, :, 0:CH] = code_ref[:, i, :]
    p1[...] = jnp.zeros(p1.shape, F32)
    p2[...] = jnp.zeros(p2.shape, F32)
    bsum[...] = jnp.zeros(bsum.shape, F32)

    drain(stat_r.at[pl.ds(0, 3)], st_rsem)
    for p in range(PT):
        r, l = p // 3, (p % 3) * QT
        sums = [stat_r[d, r : r + 1, l : l + QT] for d in range(4)]
        spreads = [stat_r[d, 4 + r : 5 + r, l : l + QT] for d in range(4)]
        mean = (sums[0] + sums[1] + sums[2] + sums[3]) * (1.0 / ALL_CH)
        spread = spreads[0] + spreads[1] + spreads[2] + spreads[3]
        for d in range(4):
            gap = sums[d] * (1.0 / CH) - mean
            spread = spread + CH * gap * gap
        mr[0:1, lanes(p)] = mean
        mr[1:2, lanes(p)] = lax.rsqrt(spread * (1.0 / ALL_CH) + 1e-05)

    def xhat(r0, p):
        v = x_ref[0, pl.ds(r0, 16), lanes(p)].astype(F32)
        return (v - mr[0:1, lanes(p)]) * mr[1:2, lanes(p)]

    forward_rows(lambda r0, p: xhat(r0, p) * gcol[pl.ds(r0, 16), :])
    for c in range(CK):
        zs[1, c] = dft_chunk(c).astype(BF).reshape(NZ, 16, LC)
        z_exchange(zs.at[1, c], zr.at[1, c], zs_sem.at[1, c], zr_sem.at[1, c])

    def second_exchange(f, c):
        z_done(zr.at[f, c], zr_sem.at[f, c])
        got = zr[f, c].reshape(256, LC)
        xs[f, c] = dot_nn(perm_ref[...], got).astype(BF).reshape(NJ, 32, LC)
        xy_exchange(xs.at[f, c], xr.at[f, c], xs_sem.at[f, c], xr_sem.at[f, c])

    def latitude_modes(f, c):
        xy_done(xr.at[f, c], xr_sem.at[f, c])
        spread = dot_nn(xr[f, c].reshape(256, LC), wide_ref[...]).astype(BF)
        return dot_nn(lat_ref[...], spread)

    def bit(code, place):
        return jnp.bitwise_and(jnp.right_shift(code, place), 1).astype(F32)

    def mode_rows(c, i):
        return slice((c * MC + i) * 128, (c * MC + i + 1) * 128)

    def masked(dst, rows, value, code, place):
        dst[rows, 0:128] = (value[0] * bit(code, place)).astype(BF)
        dst[rows, 128:256] = (value[1] * bit(code, place + 1)).astype(BF)

    def backward_chunk(c):
        freq = latitude_modes(0, c)
        for i in range(MC):
            col = slice(i * 128, (i + 1) * 128)
            masked(sg_all, mode_rows(c, i), (freq[0:128, col], freq[128:256, col]), cm[c * MC + i], 2)
        chunk = slice(c * LP, (c + 1) * LP)
        back = dot_nt(sg_all[chunk, :], m2[...])
        for i in range(MC):
            row = slice(i * 128, (i + 1) * 128)
            masked(bh_all, mode_rows(c, i), (back[row, 0:128], back[row, 128:256]), cm[c * MC + i], 0)
        grad = dot_nt(bh_all[chunk, :], m1[...]).astype(BF)
        for i in range(MC):
            row = slice(i * 128, (i + 1) * 128)
            gp[0:128, row] = grad[row, 0:128]
            gp[128:256, row] = grad[row, 128:256]
        spec = dot_nn(lati_ref[...], gp[...]).astype(BF)
        bxs[c] = dot_nn(spec, narrow_ref[...]).astype(BF).reshape(NJ, 32, LC)
        xy_exchange(bxs.at[c], bxr.at[c], bxs_sem.at[c], bxr_sem.at[c])

    def second_back(c):
        xy_done(bxr.at[c], bxr_sem.at[c])
        got = bxr[c].reshape(256, LC)
        bzs[c] = dot_nn(permi_ref[...], got).astype(BF).reshape(NZ, 16, LC)
        z_exchange(bzs.at[c], bzr.at[c], bzs_sem.at[c], bzr_sem.at[c])

    def weight_chunk(c):
        freq = latitude_modes(1, c)
        for i in range(MC):
            row = slice(i * 128, (i + 1) * 128)
            fi[row, 0:128] = freq[0:128, row].astype(BF)
            fi[row, 128:256] = freq[128:256, row].astype(BF)
        pre = dot_nn(fi[...], m1[...]) + bias[0:1, :]
        for i in range(MC):
            row = slice(i * 128, (i + 1) * 128)
            masked(hd, row, (pre[row, 0:128], pre[row, 128:256]), cm[c * MC + i], 0)
        chunk = slice(c * LP, (c + 1) * LP)
        sg, bh = sg_all[chunk, :], bh_all[chunk, :]
        p2[...] += dot_tn(hd[...], sg)
        p1[...] += dot_tn(fi[...], bh)
        bsum[0:1, :] += jnp.sum(bh.astype(F32), axis=0, keepdims=True)
        bsum[1:2, :] += jnp.sum(sg.astype(F32), axis=0, keepdims=True)

    second_exchange(0, 0)
    second_exchange(0, 1)
    backward_chunk(0)
    second_exchange(0, 2)
    backward_chunk(1)
    second_back(0)
    backward_chunk(2)
    second_back(1)
    second_exchange(1, 0)
    second_back(2)
    second_exchange(1, 1)
    weight_chunk(0)
    second_exchange(1, 2)
    weight_chunk(1)
    weight_chunk(2)

    for s, src in ((0, p1), (4, p2)):
        real = src[0:CH, 0:128] + src[128 : 128 + CH, 128:256]
        imag = src[0:CH, 128:256] - src[128 : 128 + CH, 0:128]
        rw[s, 0:48] = real[0:48]
        rw[s + 1, 0:48] = real[48:96]
        rw[s + 2, 0:48] = imag[0:48]
        rw[s + 3, 0:48] = imag[48:96]
    for s in range(NJ):
        rw[s, 48:56] = jnp.zeros((8, 128), F32)
    rw[0, 48:49] = bsum[0:1, 0:128]
    rw[0, 49:50] = bsum[0:1, 128:256]
    rw[0, 50:51] = bsum[1:2, 0:128]
    rw[0, 51:52] = bsum[1:2, 128:256]
    xy_exchange(rw, rr1, r1_ssem, r1_rsem)

    def inverse_chunk(c):
        z_done(bzr.at[c], bzr_sem.at[c])
        got = bzr[c].reshape(256, LC)
        vbuf[pl.ds(c * LC, LC), :] = dot_tn(got, inv_ref[...])

    inverse_chunk(0)

    xy_done(rr1, r1_rsem)
    part = rr1[0]
    for s in range(1, NJ):
        part = part + rr1[s]
    rs[...] = part.reshape(NP_, 8, 128)
    owner = (lax.rem(z, 2) == 0) & (z < 2 * NP_)
    piece = z // 2
    for t in range(NP_):
        @pl.when(z != 2 * t)
        def _():
            remote(rs.at[t], rr2.at[z], r2_ssem, r2_rsem, {"lat": base_z + 8 * t})

    @pl.when(owner)
    def _():
        rr2[z] = rs[piece]
        z_done(rr2, r2_rsem)
        total = rr2[0]
        for s in range(1, NZ):
            total = total + rr2[s]
        rt[...] = total
        rr2b[piece] = total

        def send(t):
            _, dev = z_step(t)
            remote(rt, rr2b.at[piece], r2b_ssem, r2b_rsem, dev)

        each(NZ - 1, send)

    inverse_chunk(1)

    @pl.when(owner)
    def _():
        drain(rr2b.at[pl.ds(0, NP_ - 1)], r2b_rsem)

    @pl.when(jnp.logical_not(owner))
    def _():
        drain(rr2b, r2b_rsem)

    xy_share(rr2b, rr3, r3_ssem, r3_rsem)

    inverse_chunk(2)

    hacc[...] = jnp.zeros(hacc.shape, F32)
    cacc[...] = jnp.zeros(cacc.shape, F32)

    def inverse_rows(r):
        r0 = pl.multiple_of(r * 16, 16)
        re, im = [], []
        for i in range(PT):
            rows = pl.ds(pl.multiple_of(i * CH + r0, 16), 16)
            vr = vbuf[rows, 0:QT]
            vi = vbuf[rows, QT : 2 * QT]
            c = tw_ref[i : i + 1, :]
            w = tw_ref[PT + i : PT + i + 1, :]
            re.append(vr * c - vi * w)
            im.append(None if i in (0, 6) else vr * w + vi * c)
        s = [None] + [re[i] + re[PT - i] for i in range(1, 6)]
        t = [None] + [im[i] - im[PT - i] for i in range(1, 6)]
        real, imag = real12(re[0], re[6], s, t)
        column = gcol[pl.ds(r0, 16), :]
        for p in range(PT):
            k = p if p <= 6 else PT - p
            v = real[k]
            if imag[k] is not None:
                v = v + imag[k] if p <= 6 else v - imag[k]
            v = v * column
            gbuf[pl.ds(r0, 16), lanes(p)] = v
            hacc[:, lanes(p)] += v
            cacc[:, lanes(p)] += v * xhat(r0, p)

    each(CH // 16, inverse_rows)
    for p in range(PT):
        r, l = p // 3, (p % 3) * QT
        tail_s[r : r + 1, l : l + QT] = jnp.sum(hacc[:, lanes(p)], axis=0, keepdims=True)
        tail_s[4 + r : 5 + r, l : l + QT] = jnp.sum(cacc[:, lanes(p)], axis=0, keepdims=True)
    chan_share(tail_s, tail_r, tl_ssem, tl_rsem)

    xy_done(rr3, r3_rsem)
    scale = 1.0 / math.sqrt(LAT * LON / 2)

    def summed(s):
        return rr3[s, 0:6].reshape(48, 128)[:, 0:CH]

    for s, out in ((0, giw_ref), (4, gow_ref)):
        for k in range(2):
            out[0, k, 0:48] = summed(s + 2 * k) * scale
            out[0, k, 48:96] = summed(s + 2 * k + 1) * scale
    gib_ref[0, 0:2] = rr3[0, 6, 0:2, 0:CH] * scale
    gob_ref[0, 0:2] = rr3[0, 6, 2:4, 0:CH] * scale
    product = jnp.zeros((CH, CH), F32)
    for k in range(2):
        whole = jnp.concatenate([summed(2 * k), summed(2 * k + 1)], axis=0)
        product = product + whole * iw_ref[0, k].astype(F32)
    column = jnp.sum(product, axis=1, keepdims=True)
    as_row = jnp.sum(diag * column, axis=0, keepdims=True)
    gg_ref[...] = as_row * (1.0 / math.sqrt(LAT * LON)) / gain_ref[...]

    drain(tail_r.at[pl.ds(0, 3)], tl_rsem)
    for p in range(PT):
        r, l = p // 3, (p % 3) * QT
        for k in range(2):
            q = 4 * k + r
            total = tail_r[0, q : q + 1, l : l + QT]
            for d in range(1, 4):
                total = total + tail_r[d, q : q + 1, l : l + QT]
            mr[2 + k : 3 + k, lanes(p)] = total * (1.0 / ALL_CH)

    def finish_rows(r):
        r0 = pl.multiple_of(r * 16, 16)
        for p in range(PT):
            g = gbuf[pl.ds(r0, 16), lanes(p)]
            v = g - mr[2:3, lanes(p)] - xhat(r0, p) * mr[3:4, lanes(p)]
            gin_ref[0, pl.ds(r0, 16), lanes(p)] = (v * mr[1:2, lanes(p)]).astype(BF)

    each(CH // 16, finish_rows)

    for c in range(CK):
        for f in range(2):
            z_done(zs.at[f, c], zs_sem.at[f, c])
            xy_done(xs.at[f, c], xs_sem.at[f, c])
        xy_done(bxs.at[c], bxs_sem.at[c])
        z_done(bzs.at[c], bzs_sem.at[c])
    drain(stat_r.at[pl.ds(0, 3)], st_ssem)
    drain(tail_r.at[pl.ds(0, 3)], tl_ssem)
    xy_done(rw, r1_ssem)
    xy_done(rr3, r3_ssem)

    @pl.when(owner)
    def _():
        drain(rs.at[pl.ds(0, NP_ - 1)], r2_ssem)
        z_done(rr2, r2b_ssem)

    @pl.when(jnp.logical_not(owner))
    def _():
        drain(rs, r2_ssem)


def per_device(field, cot, gain, inner_w, inner_b, outer_w, codes):
    vm = pl.BlockSpec(memory_space=pltpu.VMEM)
    tabs = [jnp.asarray(t) for t in tables()]
    S = jax.ShapeDtypeStruct
    dma = pltpu.SemaphoreType.DMA
    V = pltpu.VMEM
    scratch = [
        V((PT * CH, 2 * QT), BF),
        V((2, CK, NZ, 16, LC), BF), V((2, CK, NZ, 16, LC), BF),
        V((2, CK, NJ, 32, LC), BF), V((2, CK, NJ, 32, LC), BF),
        V((CK, NJ, 32, LC), BF), V((CK, NJ, 32, LC), BF),
        V((CK, NZ, 16, LC), BF), V((CK, NZ, 16, LC), BF),
        V((8, 768), F32), V((4, 8, 768), F32), V((8, 768), F32), V((4, 8, 768), F32),
        V((8, LON), F32), V((CH, 1), F32),
        V((256, 256), BF), V((256, 256), BF), V((8, 256), F32), V((PT, 128, 128), jnp.int32),
        V((PT * 128, 256), BF), V((PT * 128, 256), BF), V((LP, 256), BF), V((LP, 256), BF),
        V((256, LP), BF), V((256, 256), F32), V((256, 256), F32), V((8, 256), F32),
        V((PT * CH, 2 * QT), F32), V((CH, LON), F32), V((16, LON), F32), V((16, LON), F32),
        V((NJ, RW, 128), F32), V((NJ, RW, 128), F32), V((NP_, 8, 128), F32), V((NZ, 8, 128), F32),
        V((8, 128), F32), V((NP_, 8, 128), F32), V((NJ, NP_, 8, 128), F32),
        dma((2, CK)), dma((2, CK)), dma((2, CK)), dma((2, CK)),
        dma((CK,)), dma((CK,)), dma((CK,)), dma((CK,)),
    ] + [dma(())] * 12
    outs = pl.pallas_call(
        kernel,
        out_shape=(
            S((1, CH, LON), BF),
            S((1, 2, CH, CH), F32),
            S((1, 2, CH), F32),
            S((1, 2, CH, CH), F32),
            S((1, 2, CH), F32),
            S((1, CH), F32),
        ),
        in_specs=[vm] * 16,
        out_specs=(vm,) * 6,
        scratch_shapes=scratch,
        compiler_params=pltpu.CompilerParams(
            collective_id=0, has_side_effects=True, vmem_limit_bytes=56 * 2**20
        ),
        name="mixing_backward",
    )(field, cot, gain.reshape(1, CH), inner_w, inner_b, outer_w, codes, *tabs)
    return outs[:5] + (outs[5].reshape(CH),)


def solution(mesh):
    in_specs = (
        P("lat", "chan", None),
        P("lat", "chan", None),
        P("chan"),
        P("chan", None, None, None),
        P("chan", None, None),
        P("chan", None, None, None),
        P(None, "lat", "chan"),
    )
    out_specs = (
        P("lat", "chan", None),
        P("chan", None, None, None),
        P("chan", None, None),
        P("chan", None, None, None),
        P("chan", None, None),
        P("chan"),
    )
    return jax.shard_map(
        per_device, mesh=mesh, in_specs=in_specs, out_specs=out_specs, check_vma=False
    )
```

time: 1530 us -> 123 us (0.08)
  waiting for transfers between devices: 931 us -> 0 us
  blocking collectives: 386 us -> 0 us
  Pallas kernels: 0 us -> 115 us
  local copies, waits for them, and re-layouts: 79.6 us -> 7.42 us
  matrix products: 46.1 us -> 0 us
  starting transfers between devices: 34.8 us -> 0 us
  other arithmetic: 28.6 us -> 0 us
    psum x1 -> x0, waiting for transfers between devices: 843 us -> none  [per_device(): lax.psum((inner_local, ishift_local, outer_local, oshift_local, gain_loca...]
    psum x4 -> x0, blocking collectives: 386 us -> none  [the longest x1 353 us: per_device(): lax.psum((inner_local, ishift_local, outer_local, oshift_local, gain_loca...]
    pallas_call x0 -> x1, Pallas kernels: none -> 115 us  [per_device(): pl.pallas_call(kernel, out_shape=(S((1, CH, LON), BF), S((1, 2, CH, CH),...]
    all_to_all x3 -> x0, waiting for transfers between devices: 88.6 us -> none  [the longest x1 35.5 us: per_device(): lax.all_to_all(back_pencil, 'lat', split_axis=0, concat_axis=1, tiled=True)]
    dot_general x22 -> x0, matrix products: 37.5 us -> none  [the longest x2 5.69 us: longitude_forward(): jnp.einsum('lcaq,qj->ljac', turn_imag, cos_large, precision=exact_mode)]
    all_to_all x3 -> x0, starting transfers between devices: 34.7 us -> none  [the longest x1 22 us: per_device(): lax.all_to_all(to_slab(cotangent.astype(jnp.float32), cot_weight), 'lat',...]
    concatenate x5 -> x0, local copies, waits for them, and re-layouts: 22.3 us -> none  [the longest x2 17.9 us: to_slab(): jnp.concatenate([slab_real * weight, slab_imag * weight], axis=2)]
    unnamed x2 -> x0, other arithmetic: 18.7 us -> none
  transfers between devices with their start and end apart: 4 -> 0, of which waited for: 4 -> 0; matrix products, arithmetic and copies ran while one was open for 1% -> 0% of each run, Pallas kernels for 0% -> 0%
where the time goes in v1:
time: 123 us
  Pallas kernels  115 us (93%)
  local copies, waits for them, and re-layouts  7.42 us (6%)
    pallas_call x1, Pallas kernels, per_device(): pl.pallas_call(kernel, out_shape=(S((1, CH, LON), BF), S((1, 2, CH, CH),...  115 us
    unnamed x17, local copies, waits for them, and re-layouts  7.42 us

profile of v1, /device:TPU:2, one launch (start us, length us, event | category | flops | bytes accessed | tf_op | source)
XLA Modules:
  0.0 122.9 jit_solution(6726433498506041289)
XLA Ops:
  0.6 2.4 %copy.22.code_ref = s32[128,12,96]{2,1,0:T(8,128)} copy(s32[128,12,96]{0,2,1:T(8,128)} %param.22) | data formatting | bytes 1179648 | tf_op args[6]
  3.1 114.8 %mixing_backward.1 = (bf16[1,96,3072]{2,1,0:T(8,128)(2,1)}, f32[1,2,96,96]{3,2,1,0:T(8,128)}, f32[1,2,96]{2,1,0:T(2,128)}, f32[1,2,96,96]{3,2,1,0:T(8,128)}, f32[1,2,96]{2,1,0:T(2,128)}, /*index=5*/f32[1,96]{1,0:T(1,128)}) custom-call(bf16[1,96,3072]{2,1,0:T(8,128)(2,1)} %x_ref.1, bf16[1,96,3072]{2,1,0:T(8,128)(2,1)} %cot_ref.1, f32[1,96]{1,0:T(1,128)} %bitcast.2, ...), custom_call_target="tpu_custom_call" | custom-call | tf_op jit(solution)/shard_map/mixing_backward/pallas_call | solution.py:552
  117.9 0.0 copy-start.1
  117.9 2.0 %copy.29 = bf16[1,96,3072]{2,1,0:T(8,128)(2,1)} copy(bf16[1,96,3072]{2,1,0:T(8,128)(2,1)} %get-tuple-element.24) | data formatting | bytes 1179648
  119.9 0.0 copy-done.1
  119.9 0.0 copy-start.3
  119.9 0.0 copy-start
  119.9 0.6 copy.30
  120.5 0.0 copy-done.3
  120.5 0.6 copy.31
  121.1 0.0 copy-done
  121.1 0.0 copy-start.2
  121.1 0.6 copy.32
  121.7 0.0 copy-done.2
  121.8 0.0 copy-start.4
  121.8 0.6 copy.33
  122.3 0.1 copy-done.4
  122.4 0.5 copy.34
Async XLA Ops:
  117.9 2.0 %copy-start.1 = (f32[1,2,96,96]{3,2,1,0:T(8,128)S(1)}, f32[1,2,96,96]{3,2,1,0:T(8,128)}, u32[]{:S(2)}) copy-start(f32[1,2,96,96]{3,2,1,0:T(8,128)} %get-tuple-element.25) | copy-start | bytes 221188
  119.9 0.7 copy-start.3
  119.9 1.2 %copy-start = (f32[1,2,96,96]{3,2,1,0:T(8,128)S(1)}, f32[1,2,96,96]{3,2,1,0:T(8,128)}, u32[]{:S(2)}) copy-start(f32[1,2,96,96]{3,2,1,0:T(8,128)} %get-tuple-element.27) | copy-start | bytes 221188
  121.1 0.7 copy-start.2
  121.8 0.6 copy-start.4

commit v2 on v1

--- a/solution.py
+++ b/solution.py
@@ -25,8 +25,10 @@
 MC = PT // CK
 LC = MC * CH
 LP = MC * 128
-RW = 56
-NP_ = RW // 8
+RW = 64
+FR = 48
+NEAR = 4
+RP = RW // NEAR
 
 
 def tables():
@@ -55,7 +57,8 @@
         widen[i * CH + np.arange(CH), i * 128 + np.arange(CH)] = 1.0
     turn = 2 * np.pi * np.arange(PT)[:, None] * q[None, :] / LON
     twiddle = np.concatenate([np.cos(turn), np.sin(turn)], 0)
-    bf = [a.astype(ml_dtypes.bfloat16) for a in (fwd, inv, lat, lat.T, perm, perm.T, widen, widen.T)]
+    order = (fwd, perm @ fwd, inv, lat, lat @ perm, lat.T, perm, perm.T, widen, widen.T)
+    bf = [a.astype(ml_dtypes.bfloat16) for a in order]
     return bf + [twiddle.astype(np.float32)]
 
 
@@ -90,17 +93,20 @@
 
 
 def kernel(
-    x_ref, cot_ref, gain_ref, iw_ref, ib_ref, ow_ref, code_ref,
-    fwd_ref, inv_ref, lat_ref, lati_ref, perm_ref, permi_ref, wide_ref, narrow_ref, tw_ref,
-    gin_ref, giw_ref, gib_ref, gow_ref, gob_ref, gg_ref,
+    x_hbm, cot_hbm, code_hbm, fwd_hbm, fwdx_hbm, inv_hbm, lat_hbm, latz_hbm, lati_hbm,
+    perm_hbm, permi_hbm, wide_hbm, narrow_hbm,
+    gain_ref, iw_ref, ib_ref, ow_ref, tw_ref,
+    g_ref, cell_ref, wout_ref, bout_ref,
+    x_ref, cot_ref, code_ref, fwd_ref, fwdx_ref, inv_ref, lat_ref, latz_ref, lati_ref,
+    perm_ref, permi_ref, wide_ref, narrow_ref, load_sem,
     ybuf, zs, zr, xs, xr, bxs, bxr, bzs, bzr,
     stat_s, stat_r, tail_s, tail_r, mr, gcol,
     m1, m2, bias, cm, sg_all, bh_all, fi, hd, gp, p1, p2, bsum,
-    vbuf, gbuf, hacc, cacc,
-    rw, rr1, rs, rr2, rt, rr2b, rr3,
+    vbuf, hacc, cacc,
+    rw, rr1, rs, rr2, rt, rr3, ru, rr4, rv, rr5,
     zs_sem, zr_sem, xs_sem, xr_sem, bxs_sem, bxr_sem, bzs_sem, bzr_sem,
     st_ssem, st_rsem, tl_ssem, tl_rsem,
-    r1_ssem, r1_rsem, r2_ssem, r2_rsem, r2b_ssem, r2b_rsem, r3_ssem, r3_rsem,
+    r1_ssem, r1_rsem, r2_ssem, r2_rsem, r3_ssem, r3_rsem, r4_ssem, r4_rsem, r5_ssem, r5_rsem,
 ):
     me = lax.axis_index("lat")
     chan = lax.axis_index("chan")
@@ -123,6 +129,16 @@
         ty = lax.rem(y + lax.rem(d, 4), 4)
         return tx * 4 + ty, {"lat": tx * 64 + z * 4 + ty}
 
+    near, block = lax.rem(z, NEAR), z // NEAR
+
+    def near_step(t):
+        to = lax.rem(near + t + 1, NEAR)
+        return to, {"lat": base_z + (block * NEAR + to) * 4}
+
+    def far_step(t):
+        to = lax.rem(block + t + 1, NZ // NEAR)
+        return to, {"lat": base_z + (to * NEAR + near) * 4}
+
     def chan_step(t):
         to = lax.rem(chan + t + 1, 4)
         return to, {"chan": to}
@@ -158,21 +174,19 @@
         each(NJ - 1, send)
         dst[j] = src[j]
 
-    def xy_share(src, dst, ssem, rsem):
+    def share(step, count, place, src, dst, ssem, rsem):
         def send(t):
-            _, dev = xy_step(t)
-            remote(src, dst.at[j], ssem, rsem, dev)
-
-        each(NJ - 1, send)
-        dst[j] = src[...]
+            _, dev = step(t)
+            remote(src, dst.at[place], ssem, rsem, dev)
+
+        each(count - 1, send)
+        dst[place] = src[...]
 
     def chan_share(src, dst, ssem, rsem):
-        def send(t):
-            _, dev = chan_step(t)
-            remote(src, dst.at[chan], ssem, rsem, dev)
-
-        each(3, send)
-        dst[chan] = src[...]
+        share(chan_step, 4, chan, src, dst, ssem, rsem)
+
+    def rest(ref, count, sem):
+        drain(ref.at[pl.ds(0, count - 1)], sem)
 
     def z_done(ref, sem):
         drain(ref.at[pl.ds(0, NZ - 1)], sem)
@@ -192,6 +206,19 @@
     each(NZ - 1, greet(z_step))
     each(NJ - 1, greet(xy_step))
     each(3, greet(chan_step))
+
+    loads = [
+        pltpu.make_async_copy(src, dst, load_sem.at[k])
+        for k, (src, dst) in enumerate((
+            (cot_hbm, cot_ref), (fwd_hbm, fwd_ref), (x_hbm, x_ref), (fwdx_hbm, fwdx_ref),
+            (permi_hbm, permi_ref), (perm_hbm, perm_ref), (code_hbm, code_ref), (wide_hbm, wide_ref),
+            (lat_hbm, lat_ref), (lati_hbm, lati_ref), (narrow_hbm, narrow_ref),
+            (latz_hbm, latz_ref), (inv_hbm, inv_ref),
+        ))
+    ]
+    for load in loads:
+        load.start()
+    loads[0].wait()
 
     def lanes(p):
         return slice(p * QT, (p + 1) * QT)
@@ -221,12 +248,13 @@
 
         each(CH // 16, block)
 
-    def dft_chunk(c):
-        return dot_nt(fwd_ref[...], ybuf[pl.ds(c * LC, LC), :])
-
-    forward_rows(lambda r0, p: cot_ref[0, pl.ds(r0, 16), lanes(p)].astype(F32) * 2.0)
+    def dft_chunk(table, c):
+        return dot_nt(table[...], ybuf[pl.ds(c * LC, LC), :])
+
+    forward_rows(lambda r0, p: cot_ref[0, pl.ds(r0, 16), lanes(p)].astype(F32))
+    loads[1].wait()
     for c in range(CK):
-        out = dft_chunk(c)
+        out = dft_chunk(fwd_ref, c)
         if c == 0:
             row = lax.broadcasted_iota(jnp.int32, out.shape, 0)
             lane = lax.broadcasted_iota(jnp.int32, out.shape, 1)
@@ -237,6 +265,7 @@
             pl.semaphore_wait(barrier, NZ - 1 + NJ - 1 + 3)
         z_exchange(zs.at[0, c], zr.at[0, c], zs_sem.at[0, c], zr_sem.at[0, c])
 
+    loads[2].wait()
     for p in range(PT):
         v = x_ref[0, :, lanes(p)].astype(F32)
         total = jnp.sum(v, axis=0, keepdims=True)
@@ -260,8 +289,9 @@
     bias[0:1, 0:CH] = ib_ref[0, 0:1, :]
     bias[0:1, 128 : 128 + CH] = ib_ref[0, 1:2, :]
     cm[...] = jnp.zeros(cm.shape, jnp.int32)
+    loads[6].wait()
     for i in range(PT):
-        cm[i, :, 0:CH] = code_ref[:, i, :]
+        cm[i, :, 0:CH] = code_ref[i].T
     p1[...] = jnp.zeros(p1.shape, F32)
     p2[...] = jnp.zeros(p2.shape, F32)
     bsum[...] = jnp.zeros(bsum.shape, F32)
@@ -284,22 +314,33 @@
         return (v - mr[0:1, lanes(p)]) * mr[1:2, lanes(p)]
 
     forward_rows(lambda r0, p: xhat(r0, p) * gcol[pl.ds(r0, 16), :])
+    for k in (3, 4, 5):
+        loads[k].wait()
     for c in range(CK):
-        zs[1, c] = dft_chunk(c).astype(BF).reshape(NZ, 16, LC)
+        xs[1, c] = dft_chunk(fwdx_ref, c).astype(BF).reshape(NJ, 32, LC)
+        xy_exchange(xs.at[1, c], xr.at[1, c], xs_sem.at[1, c], xr_sem.at[1, c])
+
+    def ready_input(c):
+        xy_done(xr.at[1, c], xr_sem.at[1, c])
+        got = xr[1, c].reshape(256, LC)
+        zs[1, c] = dot_nn(permi_ref[...], got).astype(BF).reshape(NZ, 16, LC)
+
+    def send_input(c):
         z_exchange(zs.at[1, c], zr.at[1, c], zs_sem.at[1, c], zr_sem.at[1, c])
 
-    def second_exchange(f, c):
-        z_done(zr.at[f, c], zr_sem.at[f, c])
-        got = zr[f, c].reshape(256, LC)
-        xs[f, c] = dot_nn(perm_ref[...], got).astype(BF).reshape(NJ, 32, LC)
-        xy_exchange(xs.at[f, c], xr.at[f, c], xs_sem.at[f, c], xr_sem.at[f, c])
-
-    def latitude_modes(f, c):
-        xy_done(xr.at[f, c], xr_sem.at[f, c])
-        spread = dot_nn(xr[f, c].reshape(256, LC), wide_ref[...]).astype(BF)
-        return dot_nn(lat_ref[...], spread)
+    def second_exchange(c):
+        z_done(zr.at[0, c], zr_sem.at[0, c])
+        got = zr[0, c].reshape(256, LC)
+        xs[0, c] = dot_nn(perm_ref[...], got).astype(BF).reshape(NJ, 32, LC)
+        xy_exchange(xs.at[0, c], xr.at[0, c], xs_sem.at[0, c], xr_sem.at[0, c])
+
+    def latitude_modes(table, pencil):
+        spread = dot_nn(pencil.reshape(256, LC), wide_ref[...]).astype(BF)
+        return dot_nn(table[...], spread)
 
     def bit(code, place):
+        if place >= 2:
+            return jnp.bitwise_and(jnp.right_shift(code, place - 1), 2).astype(F32)
         return jnp.bitwise_and(jnp.right_shift(code, place), 1).astype(F32)
 
     def mode_rows(c, i):
@@ -310,7 +351,8 @@
         dst[rows, 128:256] = (value[1] * bit(code, place + 1)).astype(BF)
 
     def backward_chunk(c):
-        freq = latitude_modes(0, c)
+        xy_done(xr.at[0, c], xr_sem.at[0, c])
+        freq = latitude_modes(lat_ref, xr[0, c])
         for i in range(MC):
             col = slice(i * 128, (i + 1) * 128)
             masked(sg_all, mode_rows(c, i), (freq[0:128, col], freq[128:256, col]), cm[c * MC + i], 2)
@@ -332,10 +374,13 @@
         xy_done(bxr.at[c], bxr_sem.at[c])
         got = bxr[c].reshape(256, LC)
         bzs[c] = dot_nn(permi_ref[...], got).astype(BF).reshape(NZ, 16, LC)
+
+    def send_back(c):
         z_exchange(bzs.at[c], bzr.at[c], bzs_sem.at[c], bzr_sem.at[c])
 
     def weight_chunk(c):
-        freq = latitude_modes(1, c)
+        z_done(zr.at[1, c], zr_sem.at[1, c])
+        freq = latitude_modes(latz_ref, zr[1, c])
         for i in range(MC):
             row = slice(i * 128, (i + 1) * 128)
             fi[row, 0:128] = freq[0:128, row].astype(BF)
@@ -351,20 +396,27 @@
         bsum[0:1, :] += jnp.sum(bh.astype(F32), axis=0, keepdims=True)
         bsum[1:2, :] += jnp.sum(sg.astype(F32), axis=0, keepdims=True)
 
-    second_exchange(0, 0)
-    second_exchange(0, 1)
+    for c in range(CK):
+        ready_input(c)
+    second_exchange(0)
+    send_input(0)
+    second_exchange(1)
+    send_input(1)
+    for k in (7, 8, 9, 10):
+        loads[k].wait()
     backward_chunk(0)
-    second_exchange(0, 2)
+    second_exchange(2)
+    send_input(2)
     backward_chunk(1)
     second_back(0)
     backward_chunk(2)
     second_back(1)
-    second_exchange(1, 0)
+    loads[11].wait()
+    weight_chunk(0)
+    send_back(0)
     second_back(2)
-    second_exchange(1, 1)
-    weight_chunk(0)
-    second_exchange(1, 2)
     weight_chunk(1)
+    send_back(1)
     weight_chunk(2)
 
     for s, src in ((0, p1), (4, p2)):
@@ -375,60 +427,47 @@
         rw[s + 2, 0:48] = imag[0:48]
         rw[s + 3, 0:48] = imag[48:96]
     for s in range(NJ):
-        rw[s, 48:56] = jnp.zeros((8, 128), F32)
+        rw[s, 48:RW] = jnp.zeros((RW - 48, 128), F32)
     rw[0, 48:49] = bsum[0:1, 0:128]
     rw[0, 49:50] = bsum[0:1, 128:256]
     rw[0, 50:51] = bsum[1:2, 0:128]
     rw[0, 51:52] = bsum[1:2, 128:256]
     xy_exchange(rw, rr1, r1_ssem, r1_rsem)
+    send_back(2)
 
     def inverse_chunk(c):
         z_done(bzr.at[c], bzr_sem.at[c])
         got = bzr[c].reshape(256, LC)
         vbuf[pl.ds(c * LC, LC), :] = dot_tn(got, inv_ref[...])
 
+    loads[12].wait()
+
+    def total(ref, count):
+        part = ref[0]
+        for s in range(1, count):
+            part = part + ref[s]
+        return part
+
+    xy_done(rr1, r1_rsem)
+    rs[...] = total(rr1, NJ).reshape(NEAR, RP, 128)
+
+    def send_near(t):
+        to, dev = near_step(t)
+        remote(rs.at[to], rr2.at[near], r2_ssem, r2_rsem, dev)
+
+    each(NEAR - 1, send_near)
+    rr2[near] = rs[near]
+    rest(rr2, NEAR, r2_rsem)
+    rt[...] = total(rr2, NEAR)
+    share(far_step, NZ // NEAR, block, rt, rr3, r3_ssem, r3_rsem)
     inverse_chunk(0)
-
-    xy_done(rr1, r1_rsem)
-    part = rr1[0]
-    for s in range(1, NJ):
-        part = part + rr1[s]
-    rs[...] = part.reshape(NP_, 8, 128)
-    owner = (lax.rem(z, 2) == 0) & (z < 2 * NP_)
-    piece = z // 2
-    for t in range(NP_):
-        @pl.when(z != 2 * t)
-        def _():
-            remote(rs.at[t], rr2.at[z], r2_ssem, r2_rsem, {"lat": base_z + 8 * t})
-
-    @pl.when(owner)
-    def _():
-        rr2[z] = rs[piece]
-        z_done(rr2, r2_rsem)
-        total = rr2[0]
-        for s in range(1, NZ):
-            total = total + rr2[s]
-        rt[...] = total
-        rr2b[piece] = total
-
-        def send(t):
-            _, dev = z_step(t)
-            remote(rt, rr2b.at[piece], r2b_ssem, r2b_rsem, dev)
-
-        each(NZ - 1, send)
-
+    rest(rr3, NZ // NEAR, r3_rsem)
+    ru[...] = total(rr3, NZ // NEAR)
+    share(near_step, NEAR, near, ru, rr4, r4_ssem, r4_rsem)
+    rest(rr4, NEAR, r4_rsem)
+    rv[...] = rr4[...].reshape(RW, 128)
+    share(xy_step, NJ, j, rv, rr5, r5_ssem, r5_rsem)
     inverse_chunk(1)
-
-    @pl.when(owner)
-    def _():
-        drain(rr2b.at[pl.ds(0, NP_ - 1)], r2b_rsem)
-
-    @pl.when(jnp.logical_not(owner))
-    def _():
-        drain(rr2b, r2b_rsem)
-
-    xy_share(rr2b, rr3, r3_ssem, r3_rsem)
-
     inverse_chunk(2)
 
     hacc[...] = jnp.zeros(hacc.shape, F32)
@@ -455,7 +494,7 @@
             if imag[k] is not None:
                 v = v + imag[k] if p <= 6 else v - imag[k]
             v = v * column
-            gbuf[pl.ds(r0, 16), lanes(p)] = v
+            g_ref[pl.ds(r0, 16), lanes(p)] = v
             hacc[:, lanes(p)] += v
             cacc[:, lanes(p)] += v * xhat(r0, p)
 
@@ -466,25 +505,18 @@
         tail_s[4 + r : 5 + r, l : l + QT] = jnp.sum(cacc[:, lanes(p)], axis=0, keepdims=True)
     chan_share(tail_s, tail_r, tl_ssem, tl_rsem)
 
-    xy_done(rr3, r3_rsem)
+    xy_done(rr5, r5_rsem)
     scale = 1.0 / math.sqrt(LAT * LON / 2)
-
-    def summed(s):
-        return rr3[s, 0:6].reshape(48, 128)[:, 0:CH]
-
-    for s, out in ((0, giw_ref), (4, gow_ref)):
+    for s in range(4):
         for k in range(2):
-            out[0, k, 0:48] = summed(s + 2 * k) * scale
-            out[0, k, 48:96] = summed(s + 2 * k + 1) * scale
-    gib_ref[0, 0:2] = rr3[0, 6, 0:2, 0:CH] * scale
-    gob_ref[0, 0:2] = rr3[0, 6, 2:4, 0:CH] * scale
+            wout_ref[s, k * 48 : (k + 1) * 48] = rr5[2 * s + k, 0:48] * scale
+    bout_ref[0:4] = rr5[0, 48:52] * scale
     product = jnp.zeros((CH, CH), F32)
     for k in range(2):
-        whole = jnp.concatenate([summed(2 * k), summed(2 * k + 1)], axis=0)
-        product = product + whole * iw_ref[0, k].astype(F32)
+        product = product + wout_ref[k, :, 0:CH] * iw_ref[0, k].astype(F32)
     column = jnp.sum(product, axis=1, keepdims=True)
     as_row = jnp.sum(diag * column, axis=0, keepdims=True)
-    gg_ref[...] = as_row * (1.0 / math.sqrt(LAT * LON)) / gain_ref[...]
+    bout_ref[4:5, 0:CH] = as_row * (1.0 / math.sqrt(LAT * LON) / scale) / gain_ref[...]
 
     drain(tail_r.at[pl.ds(0, 3)], tl_rsem)
     for p in range(PT):
@@ -495,15 +527,7 @@
             for d in range(1, 4):
                 total = total + tail_r[d, q : q + 1, l : l + QT]
             mr[2 + k : 3 + k, lanes(p)] = total * (1.0 / ALL_CH)
-
-    def finish_rows(r):
-        r0 = pl.multiple_of(r * 16, 16)
-        for p in range(PT):
-            g = gbuf[pl.ds(r0, 16), lanes(p)]
-            v = g - mr[2:3, lanes(p)] - xhat(r0, p) * mr[3:4, lanes(p)]
-            gin_ref[0, pl.ds(r0, 16), lanes(p)] = (v * mr[1:2, lanes(p)]).astype(BF)
-
-    each(CH // 16, finish_rows)
+    cell_ref[...] = mr[...]
 
     for c in range(CK):
         for f in range(2):
@@ -514,25 +538,41 @@
     drain(stat_r.at[pl.ds(0, 3)], st_ssem)
     drain(tail_r.at[pl.ds(0, 3)], tl_ssem)
     xy_done(rw, r1_ssem)
-    xy_done(rr3, r3_ssem)
-
-    @pl.when(owner)
+    rest(rr2, NEAR, r2_ssem)
+    rest(rr3, NZ // NEAR, r3_ssem)
+    rest(rr4, NEAR, r4_ssem)
+    xy_done(rr5, r5_ssem)
+
+
+def finish(
+    x_ref, g_ref, cell_ref, w_ref, b_ref, gin_ref, giw_ref, gib_ref, gow_ref, gob_ref, gg_ref
+):
+    mean, rstd = cell_ref[0:1, :], cell_ref[1:2, :]
+    normed = (x_ref[0].astype(F32) - mean) * rstd
+    value = g_ref[...] - cell_ref[2:3, :] - normed * cell_ref[3:4, :]
+    gin_ref[0] = (value * rstd).astype(BF)
+
+    @pl.when(pl.program_id(0) == 0)
     def _():
-        drain(rs.at[pl.ds(0, NP_ - 1)], r2_ssem)
-        z_done(rr2, r2b_ssem)
-
-    @pl.when(jnp.logical_not(owner))
-    def _():
-        drain(rs, r2_ssem)
+        for k in range(2):
+            giw_ref[0, k] = w_ref[k, :, 0:CH]
+            gow_ref[0, k] = w_ref[2 + k, :, 0:CH]
+        gib_ref[0] = b_ref[0:2, 0:CH]
+        gob_ref[0] = b_ref[2:4, 0:CH]
+        gg_ref[...] = b_ref[4:5, 0:CH]
 
 
 def per_device(field, cot, gain, inner_w, inner_b, outer_w, codes):
     vm = pl.BlockSpec(memory_space=pltpu.VMEM)
-    tabs = [jnp.asarray(t) for t in tables()]
+    hbm = pl.BlockSpec(memory_space=pl.ANY)
+    *tabs, twiddle = [jnp.asarray(t) for t in tables()]
+    codes = codes.transpose(1, 2, 0)
     S = jax.ShapeDtypeStruct
     dma = pltpu.SemaphoreType.DMA
     V = pltpu.VMEM
-    scratch = [
+    loaded = [V(a.shape, a.dtype) for a in (field, cot, codes, *tabs)]
+    scratch = loaded + [
+        dma((len(loaded),)),
         V((PT * CH, 2 * QT), BF),
         V((2, CK, NZ, 16, LC), BF), V((2, CK, NZ, 16, LC), BF),
         V((2, CK, NJ, 32, LC), BF), V((2, CK, NJ, 32, LC), BF),
@@ -543,14 +583,36 @@
         V((256, 256), BF), V((256, 256), BF), V((8, 256), F32), V((PT, 128, 128), jnp.int32),
         V((PT * 128, 256), BF), V((PT * 128, 256), BF), V((LP, 256), BF), V((LP, 256), BF),
         V((256, LP), BF), V((256, 256), F32), V((256, 256), F32), V((8, 256), F32),
-        V((PT * CH, 2 * QT), F32), V((CH, LON), F32), V((16, LON), F32), V((16, LON), F32),
-        V((NJ, RW, 128), F32), V((NJ, RW, 128), F32), V((NP_, 8, 128), F32), V((NZ, 8, 128), F32),
-        V((8, 128), F32), V((NP_, 8, 128), F32), V((NJ, NP_, 8, 128), F32),
+        V((PT * CH, 2 * QT), F32), V((16, LON), F32), V((16, LON), F32),
+        V((NJ, RW, 128), F32), V((NJ, RW, 128), F32),
+        V((NEAR, RP, 128), F32), V((NEAR, RP, 128), F32), V((RP, 128), F32),
+        V((NZ // NEAR, RP, 128), F32), V((RP, 128), F32), V((NEAR, RP, 128), F32),
+        V((RW, 128), F32), V((NJ, RW, 128), F32),
         dma((2, CK)), dma((2, CK)), dma((2, CK)), dma((2, CK)),
         dma((CK,)), dma((CK,)), dma((CK,)), dma((CK,)),
-    ] + [dma(())] * 12
+    ] + [dma(())] * 14
+    gain_row = gain.reshape(1, CH)
+    grad, cells, weights, small = pl.pallas_call(
+        kernel,
+        out_shape=(
+            S((CH, LON), F32),
+            S((8, LON), F32),
+            S((4, CH, 128), F32),
+            S((8, 128), F32),
+        ),
+        in_specs=[hbm] * 13 + [vm] * 5,
+        out_specs=(vm,) * 4,
+        scratch_shapes=scratch,
+        compiler_params=pltpu.CompilerParams(
+            collective_id=0, has_side_effects=True, vmem_limit_bytes=56 * 2**20
+        ),
+        name="mixing_backward",
+    )(field, cot, codes, *tabs, gain_row, inner_w, inner_b, outer_w, twiddle)
+    def fixed(*shape):
+        return pl.BlockSpec(shape, lambda i: (0,) * len(shape))
+
     outs = pl.pallas_call(
-        kernel,
+        finish,
         out_shape=(
             S((1, CH, LON), BF),
             S((1, 2, CH, CH), F32),
@@ -559,14 +621,25 @@
             S((1, 2, CH), F32),
             S((1, CH), F32),
         ),
-        in_specs=[vm] * 16,
-        out_specs=(vm,) * 6,
-        scratch_shapes=scratch,
-        compiler_params=pltpu.CompilerParams(
-            collective_id=0, has_side_effects=True, vmem_limit_bytes=56 * 2**20
+        grid=(CH // FR,),
+        in_specs=[
+            pl.BlockSpec((1, FR, LON), lambda i: (0, i, 0)),
+            pl.BlockSpec((FR, LON), lambda i: (i, 0)),
+            fixed(8, LON),
+            fixed(4, CH, 128),
+            fixed(8, 128),
+        ],
+        out_specs=(
+            pl.BlockSpec((1, FR, LON), lambda i: (0, i, 0)),
+            fixed(1, 2, CH, CH),
+            fixed(1, 2, CH),
+            fixed(1, 2, CH, CH),
+            fixed(1, 2, CH),
+            fixed(1, CH),
         ),
-        name="mixing_backward",
-    )(field, cot, gain.reshape(1, CH), inner_w, inner_b, outer_w, codes, *tabs)
+        compiler_params=pltpu.CompilerParams(dimension_semantics=("arbitrary",)),
+        name="finish",
+    )(field, grad, cells, weights, small)
     return outs[:5] + (outs[5].reshape(CH),)
 
 

time: 123 us -> 114 us (0.927)
  local copies, waits for them, and re-layouts: 7.42 us -> 0 us
  Pallas kernels: 115 us -> 113 us
    unnamed x17 -> x0, local copies, waits for them, and re-layouts: 7.42 us -> none
    pallas_call x1 -> x2, Pallas kernels: 115 us -> 113 us  [the longest x1 111 us: per_device(): pl.pallas_call(kernel, out_shape=(S((CH, LON), F32), S((8, LON), F32), S(...]
where the time goes in v2:
time: 114 us
  Pallas kernels  113 us (99%)
    pallas_call x1, Pallas kernels, per_device(): pl.pallas_call(kernel, out_shape=(S((CH, LON), F32), S((8, LON), F32), S(...  111 us
    pallas_call x1, Pallas kernels, per_device(): pl.pallas_call(finish, out_shape=(S((1, CH, LON), BF), S((1, 2, CH, CH),...  2.5 us

profile of v2, /device:TPU:2, one launch (start us, length us, event | category | flops | bytes accessed | tf_op | source)
XLA Modules:
  0.0 114.0 jit_solution(15752379471058846035)
XLA Ops:
  0.6 110.8 %mixing_backward.1 = (f32[96,3072]{1,0:T(8,128)}, f32[8,3072]{1,0:T(8,128)}, f32[4,96,128]{2,1,0:T(8,128)}, f32[8,128]{1,0:T(8,128)}) custom-call(bf16[1,96,3072]{2,1,0:T(8,128)(2,1)} %x_ref.1, bf16[1,96,3072]{2,1,0:T(8,128)(2,1)} %cot_hbm.1, s32[12,96,128]{2,1,0:T(8,128)} %bitcast.3, bf16[256,512]{1,0:T(8,128)(2,1)} %constant.20.clone.fwd_hbm.inv_hbm, ...), custom_call_target="tpu_custom_call" | custom-call | tf_op jit(solution)/shard_map/mixing_backward/pallas_call | solution.py:595
  111.5 2.5 %finish.1 = (bf16[1,96,3072]{2,1,0:T(8,128)(2,1)}, f32[1,2,96,96]{3,2,1,0:T(8,128)}, f32[1,2,96]{2,1,0:T(2,128)}, f32[1,2,96,96]{3,2,1,0:T(8,128)}, f32[1,2,96]{2,1,0:T(2,128)}, /*index=5*/f32[1,96]{1,0:T(1,128)}) custom-call(bf16[1,96,3072]{2,1,0:T(8,128)(2,1)} %x_ref.1, f32[96,3072]{1,0:T(8,128)} %get-tuple-element.16.g_ref, ...), custom_call_target="tpu_custom_call" | custom-call | tf_op jit(solution)/shard_map/finish/pallas_call | solution.py:614

commit v3 on v2

--- a/solution.py
+++ b/solution.py
@@ -25,7 +25,7 @@
 MC = PT // CK
 LC = MC * CH
 LP = MC * 128
-RW = 64
+RW = 48
 FR = 48
 NEAR = 4
 RP = RW // NEAR
@@ -39,8 +39,8 @@
     ang = 2 * np.pi * ((dev[:, None] * q[None, :]) % QT) / QT
     cos, sin = np.cos(ang), np.sin(ang)
     re = part[:, None] == 0
-    fwd = np.concatenate([np.where(re, cos, -sin), np.where(re, sin, cos)], 1) / math.sqrt(LON)
-    inv = np.concatenate([np.where(re, cos, -sin), np.where(re, sin, cos)], 1) / math.sqrt(LON)
+    fwd = np.concatenate([np.where(re, cos, -sin), np.where(re, sin, cos)], 1)
+    inv = np.concatenate([np.where(re, cos, -sin), np.where(re, sin, cos)], 1)
     j2, p2, z2 = np.meshgrid(np.arange(NJ), np.arange(2), np.arange(NZ), indexing="ij")
     dev2 = ((j2 // 4) * 64 + z2 * 4 + j2 % 4).reshape(-1)
     part2 = p2.reshape(-1)
@@ -56,7 +56,7 @@
     for i in range(MC):
         widen[i * CH + np.arange(CH), i * 128 + np.arange(CH)] = 1.0
     turn = 2 * np.pi * np.arange(PT)[:, None] * q[None, :] / LON
-    twiddle = np.concatenate([np.cos(turn), np.sin(turn)], 0)
+    twiddle = np.concatenate([np.cos(turn), np.sin(turn)], 0) / math.sqrt(LON)
     order = (fwd, perm @ fwd, inv, lat, lat @ perm, lat.T, perm, perm.T, widen, widen.T)
     bf = [a.astype(ml_dtypes.bfloat16) for a in order]
     return bf + [twiddle.astype(np.float32)]
@@ -203,7 +203,7 @@
 
         return one
 
-    each(NZ - 1, greet(z_step))
+    each(NZ - 1, greet(lambda t: z_step(NZ - 2 - t)))
     each(NJ - 1, greet(xy_step))
     each(3, greet(chan_step))
 
@@ -369,6 +369,8 @@
         spec = dot_nn(lati_ref[...], gp[...]).astype(BF)
         bxs[c] = dot_nn(spec, narrow_ref[...]).astype(BF).reshape(NJ, 32, LC)
         xy_exchange(bxs.at[c], bxr.at[c], bxs_sem.at[c], bxr_sem.at[c])
+        bsum[0:1, :] += jnp.sum(bh_all[chunk, :].astype(F32), axis=0, keepdims=True)
+        bsum[1:2, :] += jnp.sum(sg_all[chunk, :].astype(F32), axis=0, keepdims=True)
 
     def second_back(c):
         xy_done(bxr.at[c], bxr_sem.at[c])
@@ -393,8 +395,6 @@
         sg, bh = sg_all[chunk, :], bh_all[chunk, :]
         p2[...] += dot_tn(hd[...], sg)
         p1[...] += dot_tn(fi[...], bh)
-        bsum[0:1, :] += jnp.sum(bh.astype(F32), axis=0, keepdims=True)
-        bsum[1:2, :] += jnp.sum(sg.astype(F32), axis=0, keepdims=True)
 
     for c in range(CK):
         ready_input(c)
@@ -413,10 +413,9 @@
     second_back(1)
     loads[11].wait()
     weight_chunk(0)
-    send_back(0)
     second_back(2)
     weight_chunk(1)
-    send_back(1)
+    send_back(0)
     weight_chunk(2)
 
     for s, src in ((0, p1), (4, p2)):
@@ -426,19 +425,26 @@
         rw[s + 1, 0:48] = real[48:96]
         rw[s + 2, 0:48] = imag[0:48]
         rw[s + 3, 0:48] = imag[48:96]
-    for s in range(NJ):
-        rw[s, 48:RW] = jnp.zeros((RW - 48, 128), F32)
-    rw[0, 48:49] = bsum[0:1, 0:128]
-    rw[0, 49:50] = bsum[0:1, 128:256]
-    rw[0, 50:51] = bsum[1:2, 0:128]
-    rw[0, 51:52] = bsum[1:2, 128:256]
+    for r in range(4):
+        for k in range(3):
+            l = (r % 2) * 128 + 32 * k
+            rw[0, 3 * r + k : 3 * r + k + 1, CH:128] = bsum[r // 2 : r // 2 + 1, l : l + 32]
     xy_exchange(rw, rr1, r1_ssem, r1_rsem)
-    send_back(2)
+    send_back(1)
 
     def inverse_chunk(c):
         z_done(bzr.at[c], bzr_sem.at[c])
         got = bzr[c].reshape(256, LC)
-        vbuf[pl.ds(c * LC, LC), :] = dot_tn(got, inv_ref[...])
+        out = dot_tn(got, inv_ref[...])
+        for k in range(MC):
+            i = c * MC + k
+            vr = out[k * CH : (k + 1) * CH, 0:QT]
+            vi = out[k * CH : (k + 1) * CH, QT : 2 * QT]
+            co = tw_ref[i : i + 1, :]
+            si = tw_ref[PT + i : PT + i + 1, :]
+            vbuf[i * CH : (i + 1) * CH, 0:QT] = vr * co - vi * si
+            if i not in (0, 6):
+                vbuf[i * CH : (i + 1) * CH, QT : 2 * QT] = vr * si + vi * co
 
     loads[12].wait()
 
@@ -449,7 +455,10 @@
         return part
 
     xy_done(rr1, r1_rsem)
-    rs[...] = total(rr1, NJ).reshape(NEAR, RP, 128)
+    part = total(rr1, NJ)
+    rs[...] = jnp.zeros(rs.shape, F32)
+    for k in range(NEAR):
+        rs[k, 0:RP] = part[k * RP : (k + 1) * RP]
 
     def send_near(t):
         to, dev = near_step(t)
@@ -460,57 +469,65 @@
     rest(rr2, NEAR, r2_rsem)
     rt[...] = total(rr2, NEAR)
     share(far_step, NZ // NEAR, block, rt, rr3, r3_ssem, r3_rsem)
+    send_back(2)
     inverse_chunk(0)
+    inverse_chunk(1)
     rest(rr3, NZ // NEAR, r3_rsem)
     ru[...] = total(rr3, NZ // NEAR)
     share(near_step, NEAR, near, ru, rr4, r4_ssem, r4_rsem)
     rest(rr4, NEAR, r4_rsem)
-    rv[...] = rr4[...].reshape(RW, 128)
+    for k in range(NEAR):
+        rv[k * RP : (k + 1) * RP] = rr4[k, 0:RP]
     share(xy_step, NJ, j, rv, rr5, r5_ssem, r5_rsem)
-    inverse_chunk(1)
     inverse_chunk(2)
 
     hacc[...] = jnp.zeros(hacc.shape, F32)
     cacc[...] = jnp.zeros(cacc.shape, F32)
 
-    def inverse_rows(r):
-        r0 = pl.multiple_of(r * 16, 16)
-        re, im = [], []
-        for i in range(PT):
-            rows = pl.ds(pl.multiple_of(i * CH + r0, 16), 16)
-            vr = vbuf[rows, 0:QT]
-            vi = vbuf[rows, QT : 2 * QT]
-            c = tw_ref[i : i + 1, :]
-            w = tw_ref[PT + i : PT + i + 1, :]
-            re.append(vr * c - vi * w)
-            im.append(None if i in (0, 6) else vr * w + vi * c)
-        s = [None] + [re[i] + re[PT - i] for i in range(1, 6)]
-        t = [None] + [im[i] - im[PT - i] for i in range(1, 6)]
-        real, imag = real12(re[0], re[6], s, t)
-        column = gcol[pl.ds(r0, 16), :]
+    half_lanes = [[slice(p * QT + h * 128, p * QT + h * 128 + 128) for p in range(PT)] for h in range(2)]
+
+    for h in range(2):
+        at = half_lanes[h]
+
+        def inverse_rows(r):
+            r0 = pl.multiple_of(r * 32, 32)
+            re, im = [], []
+            for i in range(PT):
+                rows = pl.ds(pl.multiple_of(i * CH + r0, 32), 32)
+                re.append(vbuf[rows, h * 128 : h * 128 + 128])
+                im.append(None if i in (0, 6) else vbuf[rows, QT + h * 128 : QT + h * 128 + 128])
+            s = [None] + [re[i] + re[PT - i] for i in range(1, 6)]
+            t = [None] + [im[i] - im[PT - i] for i in range(1, 6)]
+            real, imag = real12(re[0], re[6], s, t)
+            column = gcol[pl.ds(r0, 32), :]
+            for p in range(PT):
+                k = p if p <= 6 else PT - p
+                v = real[k]
+                if imag[k] is not None:
+                    v = v + imag[k] if p <= 6 else v - imag[k]
+                v = v * column
+                g_ref[pl.ds(r0, 32), at[p]] = v
+                field = x_ref[0, pl.ds(r0, 32), at[p]].astype(F32)
+                w = v * ((field - mr[0:1, at[p]]) * mr[1:2, at[p]])
+                hacc[:, at[p]] += (v[0:8] + v[8:16]) + (v[16:24] + v[24:32])
+                cacc[:, at[p]] += (w[0:8] + w[8:16]) + (w[16:24] + w[24:32])
+
+        each(CH // 32, inverse_rows)
         for p in range(PT):
-            k = p if p <= 6 else PT - p
-            v = real[k]
-            if imag[k] is not None:
-                v = v + imag[k] if p <= 6 else v - imag[k]
-            v = v * column
-            g_ref[pl.ds(r0, 16), lanes(p)] = v
-            hacc[:, lanes(p)] += v
-            cacc[:, lanes(p)] += v * xhat(r0, p)
-
-    each(CH // 16, inverse_rows)
-    for p in range(PT):
-        r, l = p // 3, (p % 3) * QT
-        tail_s[r : r + 1, l : l + QT] = jnp.sum(hacc[:, lanes(p)], axis=0, keepdims=True)
-        tail_s[4 + r : 5 + r, l : l + QT] = jnp.sum(cacc[:, lanes(p)], axis=0, keepdims=True)
-    chan_share(tail_s, tail_r, tl_ssem, tl_rsem)
+            r, l = p // 3, (p % 3) * 128
+            tail_s[h, r : r + 1, l : l + 128] = jnp.sum(hacc[:, at[p]], axis=0, keepdims=True)
+            tail_s[h, 4 + r : 5 + r, l : l + 128] = jnp.sum(cacc[:, at[p]], axis=0, keepdims=True)
+        chan_share(tail_s.at[h], tail_r.at[h], tl_ssem.at[h], tl_rsem.at[h])
 
     xy_done(rr5, r5_rsem)
     scale = 1.0 / math.sqrt(LAT * LON / 2)
     for s in range(4):
         for k in range(2):
             wout_ref[s, k * 48 : (k + 1) * 48] = rr5[2 * s + k, 0:48] * scale
-    bout_ref[0:4] = rr5[0, 48:52] * scale
+    for r in range(4):
+        for k in range(3):
+            row = rr5[0, 3 * r + k : 3 * r + k + 1, CH:128]
+            bout_ref[r : r + 1, 32 * k : 32 * k + 32] = row * scale
     product = jnp.zeros((CH, CH), F32)
     for k in range(2):
         product = product + wout_ref[k, :, 0:CH] * iw_ref[0, k].astype(F32)
@@ -518,15 +535,16 @@
     as_row = jnp.sum(diag * column, axis=0, keepdims=True)
     bout_ref[4:5, 0:CH] = as_row * (1.0 / math.sqrt(LAT * LON) / scale) / gain_ref[...]
 
-    drain(tail_r.at[pl.ds(0, 3)], tl_rsem)
-    for p in range(PT):
-        r, l = p // 3, (p % 3) * QT
-        for k in range(2):
-            q = 4 * k + r
-            total = tail_r[0, q : q + 1, l : l + QT]
-            for d in range(1, 4):
-                total = total + tail_r[d, q : q + 1, l : l + QT]
-            mr[2 + k : 3 + k, lanes(p)] = total * (1.0 / ALL_CH)
+    for h in range(2):
+        drain(tail_r.at[h, pl.ds(0, 3)], tl_rsem.at[h])
+        for p in range(PT):
+            r, l = p // 3, (p % 3) * 128
+            for k in range(2):
+                q = 4 * k + r
+                whole = tail_r[h, 0, q : q + 1, l : l + 128]
+                for d in range(1, 4):
+                    whole = whole + tail_r[h, d, q : q + 1, l : l + 128]
+                mr[2 + k : 3 + k, half_lanes[h][p]] = whole * (1.0 / ALL_CH)
     cell_ref[...] = mr[...]
 
     for c in range(CK):
@@ -536,7 +554,8 @@
         xy_done(bxs.at[c], bxs_sem.at[c])
         z_done(bzs.at[c], bzs_sem.at[c])
     drain(stat_r.at[pl.ds(0, 3)], st_ssem)
-    drain(tail_r.at[pl.ds(0, 3)], tl_ssem)
+    for h in range(2):
+        drain(tail_r.at[h, pl.ds(0, 3)], tl_ssem.at[h])
     xy_done(rw, r1_ssem)
     rest(rr2, NEAR, r2_ssem)
     rest(rr3, NZ // NEAR, r3_ssem)
@@ -578,19 +597,19 @@
         V((2, CK, NJ, 32, LC), BF), V((2, CK, NJ, 32, LC), BF),
         V((CK, NJ, 32, LC), BF), V((CK, NJ, 32, LC), BF),
         V((CK, NZ, 16, LC), BF), V((CK, NZ, 16, LC), BF),
-        V((8, 768), F32), V((4, 8, 768), F32), V((8, 768), F32), V((4, 8, 768), F32),
+        V((8, 768), F32), V((4, 8, 768), F32), V((2, 8, 384), F32), V((2, 4, 8, 384), F32),
         V((8, LON), F32), V((CH, 1), F32),
         V((256, 256), BF), V((256, 256), BF), V((8, 256), F32), V((PT, 128, 128), jnp.int32),
         V((PT * 128, 256), BF), V((PT * 128, 256), BF), V((LP, 256), BF), V((LP, 256), BF),
         V((256, LP), BF), V((256, 256), F32), V((256, 256), F32), V((8, 256), F32),
-        V((PT * CH, 2 * QT), F32), V((16, LON), F32), V((16, LON), F32),
+        V((PT * CH, 2 * QT), F32), V((8, LON), F32), V((8, LON), F32),
         V((NJ, RW, 128), F32), V((NJ, RW, 128), F32),
-        V((NEAR, RP, 128), F32), V((NEAR, RP, 128), F32), V((RP, 128), F32),
-        V((NZ // NEAR, RP, 128), F32), V((RP, 128), F32), V((NEAR, RP, 128), F32),
+        V((NEAR, 16, 128), F32), V((NEAR, 16, 128), F32), V((16, 128), F32),
+        V((NZ // NEAR, 16, 128), F32), V((16, 128), F32), V((NEAR, 16, 128), F32),
         V((RW, 128), F32), V((NJ, RW, 128), F32),
         dma((2, CK)), dma((2, CK)), dma((2, CK)), dma((2, CK)),
         dma((CK,)), dma((CK,)), dma((CK,)), dma((CK,)),
-    ] + [dma(())] * 14
+    ] + [dma(()), dma(()), dma((2,)), dma((2,))] + [dma(())] * 10
     gain_row = gain.reshape(1, CH)
     grad, cells, weights, small = pl.pallas_call(
         kernel,

time: 114 us -> 110 us (0.965)
  Pallas kernels: 113 us -> 110 us
    pallas_call x1, Pallas kernels: 111 us -> 107 us  [per_device(): pl.pallas_call(kernel, out_shape=(S((CH, LON), F32), S((8, LON), F32), S(...]
where the time goes in v3:
time: 110 us
  Pallas kernels  110 us (100%)
    pallas_call x1, Pallas kernels, per_device(): pl.pallas_call(kernel, out_shape=(S((CH, LON), F32), S((8, LON), F32), S(...  107 us
    pallas_call x1, Pallas kernels, per_device(): pl.pallas_call(finish, out_shape=(S((1, CH, LON), BF), S((1, 2, CH, CH),...  2.5 us

profile of v3, /device:TPU:2, one launch (start us, length us, event | category | flops | bytes accessed | tf_op | source)
XLA Modules:
  0.0 110.2 jit_solution(13413441131423066618)
XLA Ops:
  0.6 107.0 %mixing_backward.1 = (f32[96,3072]{1,0:T(8,128)}, f32[8,3072]{1,0:T(8,128)}, f32[4,96,128]{2,1,0:T(8,128)}, f32[8,128]{1,0:T(8,128)}) custom-call(bf16[1,96,3072]{2,1,0:T(8,128)(2,1)} %x_ref.1, bf16[1,96,3072]{2,1,0:T(8,128)(2,1)} %cot_hbm.1, s32[12,96,128]{2,1,0:T(8,128)} %bitcast.3, bf16[256,512]{1,0:T(8,128)(2,1)} %constant.20.clone.fwd_hbm.inv_hbm, ...), custom_call_target="tpu_custom_call" | custom-call | tf_op jit(solution)/shard_map/mixing_backward/pallas_call | solution.py:614
  107.7 2.5 %finish.1 = (bf16[1,96,3072]{2,1,0:T(8,128)(2,1)}, f32[1,2,96,96]{3,2,1,0:T(8,128)}, f32[1,2,96]{2,1,0:T(2,128)}, f32[1,2,96,96]{3,2,1,0:T(8,128)}, f32[1,2,96]{2,1,0:T(2,128)}, /*index=5*/f32[1,96]{1,0:T(1,128)}) custom-call(bf16[1,96,3072]{2,1,0:T(8,128)(2,1)} %x_ref.1, f32[96,3072]{1,0:T(8,128)} %get-tuple-element.16.g_ref, ...), custom_call_target="tpu_custom_call" | custom-call | tf_op jit(solution)/shard_map/finish/pallas_call | solution.py:633

commit v4 on v3

--- a/solution.py
+++ b/solution.py
@@ -95,10 +95,11 @@
 def kernel(
     x_hbm, cot_hbm, code_hbm, fwd_hbm, fwdx_hbm, inv_hbm, lat_hbm, latz_hbm, lati_hbm,
     perm_hbm, permi_hbm, wide_hbm, narrow_hbm,
-    gain_ref, iw_ref, ib_ref, ow_ref, tw_ref,
-    g_ref, cell_ref, wout_ref, bout_ref,
+    gain_hbm, iw_hbm, ib_hbm, ow_hbm, tw_hbm,
+    g_hbm, cell_ref, wout_ref, bout_ref,
     x_ref, cot_ref, code_ref, fwd_ref, fwdx_ref, inv_ref, lat_ref, latz_ref, lati_ref,
-    perm_ref, permi_ref, wide_ref, narrow_ref, load_sem,
+    perm_ref, permi_ref, wide_ref, narrow_ref, gain_ref, iw_ref, ib_ref, ow_ref, tw_ref,
+    load_sem, g_ref, g_sem,
     ybuf, zs, zr, xs, xr, bxs, bxr, bzs, bzr,
     stat_s, stat_r, tail_s, tail_r, mr, gcol,
     m1, m2, bias, cm, sg_all, bh_all, fi, hd, gp, p1, p2, bsum,
@@ -213,11 +214,13 @@
             (cot_hbm, cot_ref), (fwd_hbm, fwd_ref), (x_hbm, x_ref), (fwdx_hbm, fwdx_ref),
             (permi_hbm, permi_ref), (perm_hbm, perm_ref), (code_hbm, code_ref), (wide_hbm, wide_ref),
             (lat_hbm, lat_ref), (lati_hbm, lati_ref), (narrow_hbm, narrow_ref),
-            (latz_hbm, latz_ref), (inv_hbm, inv_ref),
+            (latz_hbm, latz_ref), (inv_hbm, inv_ref), (gain_hbm, gain_ref), (iw_hbm, iw_ref),
+            (ib_hbm, ib_ref), (ow_hbm, ow_ref), (tw_hbm, tw_ref),
         ))
     ]
-    for load in loads:
+    for load in (loads[17], *loads[:17]):
         load.start()
+    loads[17].wait()
     loads[0].wait()
 
     def lanes(p):
@@ -275,6 +278,8 @@
         stat_s[4 + r : 5 + r, l : l + QT] = jnp.sum(off * off, axis=0, keepdims=True)
     chan_share(stat_s, stat_r, st_ssem, st_rsem)
 
+    for k in (13, 14, 15, 16):
+        loads[k].wait()
     diag = (
         lax.broadcasted_iota(jnp.int32, (CH, CH), 0) == lax.broadcasted_iota(jnp.int32, (CH, CH), 1)
     ).astype(F32)
@@ -382,6 +387,8 @@
 
     def weight_chunk(c):
         z_done(zr.at[1, c], zr_sem.at[1, c])
+        if c == CK - 1:
+            send_back(1)
         freq = latitude_modes(latz_ref, zr[1, c])
         for i in range(MC):
             row = slice(i * 128, (i + 1) * 128)
@@ -413,9 +420,9 @@
     second_back(1)
     loads[11].wait()
     weight_chunk(0)
+    send_back(0)
     second_back(2)
     weight_chunk(1)
-    send_back(0)
     weight_chunk(2)
 
     for s, src in ((0, p1), (4, p2)):
@@ -430,7 +437,6 @@
             l = (r % 2) * 128 + 32 * k
             rw[0, 3 * r + k : 3 * r + k + 1, CH:128] = bsum[r // 2 : r // 2 + 1, l : l + 32]
     xy_exchange(rw, rr1, r1_ssem, r1_rsem)
-    send_back(1)
 
     def inverse_chunk(c):
         z_done(bzr.at[c], bzr_sem.at[c])
@@ -519,6 +525,9 @@
             tail_s[h, 4 + r : 5 + r, l : l + 128] = jnp.sum(cacc[:, at[p]], axis=0, keepdims=True)
         chan_share(tail_s.at[h], tail_r.at[h], tl_ssem.at[h], tl_rsem.at[h])
 
+    g_copy = pltpu.make_async_copy(g_ref, g_hbm, g_sem)
+    g_copy.start()
+
     xy_done(rr5, r5_rsem)
     scale = 1.0 / math.sqrt(LAT * LON / 2)
     for s in range(4):
@@ -547,6 +556,7 @@
                 mr[2 + k : 3 + k, half_lanes[h][p]] = whole * (1.0 / ALL_CH)
     cell_ref[...] = mr[...]
 
+    g_copy.wait()
     for c in range(CK):
         for f in range(2):
             z_done(zs.at[f, c], zs_sem.at[f, c])
@@ -586,12 +596,14 @@
     hbm = pl.BlockSpec(memory_space=pl.ANY)
     *tabs, twiddle = [jnp.asarray(t) for t in tables()]
     codes = codes.transpose(1, 2, 0)
+    gain_row = gain.reshape(1, CH)
     S = jax.ShapeDtypeStruct
     dma = pltpu.SemaphoreType.DMA
     V = pltpu.VMEM
-    loaded = [V(a.shape, a.dtype) for a in (field, cot, codes, *tabs)]
+    given = (field, cot, codes, *tabs, gain_row, inner_w, inner_b, outer_w, twiddle)
+    loaded = [V(a.shape, a.dtype) for a in given]
     scratch = loaded + [
-        dma((len(loaded),)),
+        dma((len(loaded),)), V((CH, LON), F32), dma(()),
         V((PT * CH, 2 * QT), BF),
         V((2, CK, NZ, 16, LC), BF), V((2, CK, NZ, 16, LC), BF),
         V((2, CK, NJ, 32, LC), BF), V((2, CK, NJ, 32, LC), BF),
@@ -610,7 +622,6 @@
         dma((2, CK)), dma((2, CK)), dma((2, CK)), dma((2, CK)),
         dma((CK,)), dma((CK,)), dma((CK,)), dma((CK,)),
     ] + [dma(()), dma(()), dma((2,)), dma((2,))] + [dma(())] * 10
-    gain_row = gain.reshape(1, CH)
     grad, cells, weights, small = pl.pallas_call(
         kernel,
         out_shape=(
@@ -619,14 +630,14 @@
             S((4, CH, 128), F32),
             S((8, 128), F32),
         ),
-        in_specs=[hbm] * 13 + [vm] * 5,
-        out_specs=(vm,) * 4,
+        in_specs=[hbm] * len(given),
+        out_specs=(hbm,) + (vm,) * 3,
         scratch_shapes=scratch,
         compiler_params=pltpu.CompilerParams(
             collective_id=0, has_side_effects=True, vmem_limit_bytes=56 * 2**20
         ),
         name="mixing_backward",
-    )(field, cot, codes, *tabs, gain_row, inner_w, inner_b, outer_w, twiddle)
+    )(*given)
     def fixed(*shape):
         return pl.BlockSpec(shape, lambda i: (0,) * len(shape))
 

time: 110 us -> 108 us (0.982)
  Pallas kernels: 110 us -> 107 us
    pallas_call x1, Pallas kernels: 107 us -> 104 us  [per_device(): pl.pallas_call(kernel, out_shape=(S((CH, LON), F32), S((8, LON), F32), S(...]
where the time goes in v4:
time: 108 us; the launch traced here: 107 us
  Pallas kernels  107 us (99%)
    pallas_call x1, Pallas kernels, per_device(): pl.pallas_call(kernel, out_shape=(S((CH, LON), F32), S((8, LON), F32), S(...  104 us
    pallas_call x1, Pallas kernels, per_device(): pl.pallas_call(finish, out_shape=(S((1, CH, LON), BF), S((1, 2, CH, CH),...  2.5 us

profile of v4, /device:TPU:2, one launch (start us, length us, event | category | flops | bytes accessed | tf_op | source)
XLA Modules:
  0.0 107.5 jit_solution(14170256648172832136)
XLA Ops:
  0.6 104.3 %mixing_backward.1 = (f32[96,3072]{1,0:T(8,128)}, f32[8,3072]{1,0:T(8,128)}, f32[4,96,128]{2,1,0:T(8,128)}, f32[8,128]{1,0:T(8,128)}) custom-call(bf16[1,96,3072]{2,1,0:T(8,128)(2,1)} %x_ref.1, bf16[1,96,3072]{2,1,0:T(8,128)(2,1)} %cot_hbm.1, s32[12,96,128]{2,1,0:T(8,128)} %bitcast.3, bf16[256,512]{1,0:T(8,128)(2,1)} %constant.20.clone.fwd_hbm.inv_hbm, ...), custom_call_target="tpu_custom_call" | custom-call | tf_op jit(solution)/shard_map/mixing_backward/pallas_call | solution.py:625
  105.0 2.5 %finish.1 = (bf16[1,96,3072]{2,1,0:T(8,128)(2,1)}, f32[1,2,96,96]{3,2,1,0:T(8,128)}, f32[1,2,96]{2,1,0:T(2,128)}, f32[1,2,96,96]{3,2,1,0:T(8,128)}, f32[1,2,96]{2,1,0:T(2,128)}, /*index=5*/f32[1,96]{1,0:T(1,128)}) custom-call(bf16[1,96,3072]{2,1,0:T(8,128)(2,1)} %x_ref.1, f32[96,3072]{1,0:T(8,128)} %get-tuple-element.16.g_ref, ...), custom_call_target="tpu_custom_call" | custom-call | tf_op jit(solution)/shard_map/finish/pallas_call | solution.py:644

commit v5 on v4

--- a/solution.py
+++ b/solution.py
@@ -385,6 +385,24 @@
     def send_back(c):
         z_exchange(bzs.at[c], bzr.at[c], bzs_sem.at[c], bzr_sem.at[c])
 
+    def sum_parts(s, src):
+        real = src[0:CH, 0:128] + src[128 : 128 + CH, 128:256]
+        imag = src[0:CH, 128:256] - src[128 : 128 + CH, 0:128]
+        rw[s, 0:48] = real[0:48]
+        rw[s + 1, 0:48] = real[48:96]
+        rw[s + 2, 0:48] = imag[0:48]
+        rw[s + 3, 0:48] = imag[48:96]
+
+    def send_parts(outer):
+        def send(t):
+            to, dev = xy_step(t)
+
+            @pl.when((to >= 4) if outer else (to < 4))
+            def _():
+                remote(rw.at[to], rr1.at[j], r1_ssem, r1_rsem, dev)
+
+        each(NJ - 1, send)
+
     def weight_chunk(c):
         z_done(zr.at[1, c], zr_sem.at[1, c])
         if c == CK - 1:
@@ -401,6 +419,9 @@
         chunk = slice(c * LP, (c + 1) * LP)
         sg, bh = sg_all[chunk, :], bh_all[chunk, :]
         p2[...] += dot_tn(hd[...], sg)
+        if c == CK - 1:
+            sum_parts(4, p2)
+            send_parts(True)
         p1[...] += dot_tn(fi[...], bh)
 
     for c in range(CK):
@@ -425,18 +446,13 @@
     weight_chunk(1)
     weight_chunk(2)
 
-    for s, src in ((0, p1), (4, p2)):
-        real = src[0:CH, 0:128] + src[128 : 128 + CH, 128:256]
-        imag = src[0:CH, 128:256] - src[128 : 128 + CH, 0:128]
-        rw[s, 0:48] = real[0:48]
-        rw[s + 1, 0:48] = real[48:96]
-        rw[s + 2, 0:48] = imag[0:48]
-        rw[s + 3, 0:48] = imag[48:96]
+    sum_parts(0, p1)
     for r in range(4):
         for k in range(3):
             l = (r % 2) * 128 + 32 * k
             rw[0, 3 * r + k : 3 * r + k + 1, CH:128] = bsum[r // 2 : r // 2 + 1, l : l + 32]
-    xy_exchange(rw, rr1, r1_ssem, r1_rsem)
+    send_parts(False)
+    rr1[j] = rw[j]
 
     def inverse_chunk(c):
         z_done(bzr.at[c], bzr_sem.at[c])

time: 108 us -> 108 us (level)
  no operation moved by 1% of the time
where the time goes in v5:
time: 108 us; the launch traced here: 107 us
  Pallas kernels  107 us (99%)
    pallas_call x1, Pallas kernels, per_device(): pl.pallas_call(kernel, out_shape=(S((CH, LON), F32), S((8, LON), F32), S(...  104 us
    pallas_call x1, Pallas kernels, per_device(): pl.pallas_call(finish, out_shape=(S((1, CH, LON), BF), S((1, 2, CH, CH),...  2.5 us

profile of v5, /device:TPU:2, one launch (start us, length us, event | category | flops | bytes accessed | tf_op | source)
XLA Modules:
  0.0 107.4 jit_solution(7178508587372707197)
XLA Ops:
  0.6 104.2 %mixing_backward.1 = (f32[96,3072]{1,0:T(8,128)}, f32[8,3072]{1,0:T(8,128)}, f32[4,96,128]{2,1,0:T(8,128)}, f32[8,128]{1,0:T(8,128)}) custom-call(bf16[1,96,3072]{2,1,0:T(8,128)(2,1)} %x_ref.1, bf16[1,96,3072]{2,1,0:T(8,128)(2,1)} %cot_hbm.1, s32[12,96,128]{2,1,0:T(8,128)} %bitcast.3, bf16[256,512]{1,0:T(8,128)(2,1)} %constant.20.clone.fwd_hbm.inv_hbm, ...), custom_call_target="tpu_custom_call" | custom-call | tf_op jit(solution)/shard_map/mixing_backward/pallas_call | solution.py:641
  104.9 2.5 %finish.1 = (bf16[1,96,3072]{2,1,0:T(8,128)(2,1)}, f32[1,2,96,96]{3,2,1,0:T(8,128)}, f32[1,2,96]{2,1,0:T(2,128)}, f32[1,2,96,96]{3,2,1,0:T(8,128)}, f32[1,2,96]{2,1,0:T(2,128)}, /*index=5*/f32[1,96]{1,0:T(1,128)}) custom-call(bf16[1,96,3072]{2,1,0:T(8,128)(2,1)} %x_ref.1, f32[96,3072]{1,0:T(8,128)} %get-tuple-element.16.g_ref, ...), custom_call_target="tpu_custom_call" | custom-call | tf_op jit(solution)/shard_map/finish/pallas_call | solution.py:660
